TPU v7x, 32 devices: a whole 2x2x4 slice. The times are simulated.
32 devices in a mesh: rows: 16 (over z, y, x), cls: 2 (over core).
Axes of the slice: x: 2, y: 2, z: 4, core: 2. Of those that a mesh axis runs over, the one named last changes fastest.
Arguments:
- logits: float32 [65536, 1024], P('rows', 'cls'), may hold values from -24 to 360, as said below
- leaf_index: int32 [65536], P('rows'), may hold values from 0 to 127
- labels: int32 [65536], P('rows'), may hold values from 0 to 1023
Outputs:
- leaf_values: float32 [128, 1024], P(None, 'cls')
- updated: float32 [65536, 1024], P('rows', 'cls')
Inputs may be any that keep to these rules, and one draw needn't show every extreme that they name: `logits`: raw scores of a model in training.
All inputs are finite; a program needn't handle non-finite values.
Results may differ from a plain program's by a relative error of at most 0.0003.
Values sent between devices are 32-bit elements; how exact they have to be, the bound alone decides.
No kernel may reach another device: no remote copies, remote signals or barrier semaphores. Data moves between devices by JAX's collectives and lax.ppermute only.
A program may use at most 64 MiB of HBM per device.

v0:
```python
import jax
import jax.numpy as jnp
from jax import lax
from jax.sharding import PartitionSpec as P

LEAVES = 128


def per_device(logits, leaf_index, labels):
    row_count, class_width = logits.shape
    peak = lax.pmax(jnp.max(logits, axis=1, keepdims=True), "cls")
    expo = jnp.exp(logits - peak)
    total = lax.psum(jnp.sum(expo, axis=1, keepdims=True), "cls")
    prob = expo / total
    offset = lax.axis_index("cls") * class_width
    classes = offset + jnp.arange(class_width, dtype=jnp.int32)[None, :]
    grad = prob - (labels[:, None] == classes).astype(jnp.float32)
    hess = prob * (1.0 - prob)
    leaves = jnp.arange(LEAVES, dtype=jnp.int32)[None, :]
    onehot = (leaf_index[:, None] == leaves).astype(jnp.float32)
    dims = (((0,), (0,)), ((), ()))
    g_part = lax.dot_general(
        onehot, grad, dims, precision=lax.Precision.HIGHEST, preferred_element_type=jnp.float32
    )
    h_part = lax.dot_general(
        onehot, hess, dims, precision=lax.Precision.HIGHEST, preferred_element_type=jnp.float32
    )
    g_sum, h_sum = lax.psum((g_part, h_part), "rows")
    leaf_values = -0.3 * g_sum / (h_sum + 1.0)
    updated = logits + jnp.dot(
        onehot, leaf_values, precision=lax.Precision.HIGHEST, preferred_element_type=jnp.float32
    )
    return (leaf_values, updated)


def solution(mesh):
    return jax.shard_map(
        per_device,
        mesh=mesh,
        in_specs=(P("rows", "cls"), P("rows"), P("rows")),
        out_specs=(P(None, "cls"), P("rows", "cls")),
        check_vma=False,
    )
```

profile of v0, /device:TPU:0, one launch (start us, length us, event | category | flops | bytes accessed | tf_op | source)
XLA Modules:
  0.0 171.0 jit_solution(13420929234115800890)
XLA Ops:
  7.2 0.0 all-reduce.3.cloned.1.call-start
  7.2 4.0 %reduce_max.9 = f32[4096]{0:T(1024)S(1)} reduce(f32[4096,512]{1,0:T(8,128)} %param.3, f32[]{:T(128)} %constant.6.clone.1), dimensions={1}, to_apply=%region_0.0 | reduce | flops 2093056 | bytes 8404996 | tf_op jit(solution)/shard_map/reduce_max | solution.py:11
  11.2 3.6 %pmax.7 = f32[4096]{0:T(1024)S(1)} all-reduce(f32[4096]{0:T(1024)S(1)} %reduce_max.9), channel_id=1, replica_groups=mesh['rows'=16,'cls'=2] {'cls'}, use_global_device_ids=true, to_apply=%region_1.0 | all-reduce | flops 4096 | bytes 32768 | tf_op jit(solution)/shard_map/pmax | solution.py:11
  14.9 4.6 %fusion.6 = f32[4096]{0:T(1024)S(1)} fusion(f32[4096,512]{1,0:T(8,128)} %param.3, f32[4096]{0:T(1024)S(1)} %pmax.7), kind=kLoop, calls=%fused_computation.8 | loop fusion | flops 4190208 | bytes 8421376 | tf_op jit(solution)/shard_map/reduce_sum | solution.py:13
  19.5 3.4 %psum.21 = f32[4096]{0:T(1024)S(1)} all-reduce(f32[4096]{0:T(1024)S(1)} %fusion.6), channel_id=1, replica_groups=mesh['rows'=16,'cls'=2] {'cls'}, use_global_device_ids=true, to_apply=%region_3.0 | all-reduce | flops 4096 | bytes 32768 | tf_op jit(solution)/shard_map/psum | solution.py:13
  22.8 0.0 copy-start.1
  22.8 5.8 %fusion.5 = f32[4096,512]{1,0:T(8,128)S(1)} fusion(f32[4096,512]{1,0:T(8,128)} %param.3, f32[4096]{0:T(1024)S(1)} %psum.21, f32[4096]{0:T(1024)S(1)} %pmax.7), kind=kLoop, calls=%fused_computation.7 | loop fusion | flops 4194304 | bytes 16809984 | tf_op jit(solution)/shard_map/div | solution.py:14
  28.6 0.0 copy-done.1
  28.6 0.0 copy-start.2
  28.6 7.1 %fusion = f32[128,512]{1,0:T(8,128)} fusion(f32[4096,512]{1,0:T(8,128)S(1)} %fusion.5, s32[4096]{0:T(1024)S(1)} %copy-done.1), kind=kOutput, calls=%fused_computation.1 | convolution fusion | flops 3225944064 | bytes 8667136 | tf_op jit(solution)/shard_map/dot_general | solution.py:25
  35.8 0.0 copy-done.2
  35.8 8.0 %fusion.1 = f32[128,512]{1,0:T(8,128)} fusion(f32[4096,512]{1,0:T(8,128)S(1)} %fusion.5, s32[512]{0:T(512)S(1)} %iota_add_fusion, s32[4096]{0:T(1024)S(1)} %copy-done.2, s32[4096]{0:T(1024)S(1)} %copy-done.1), kind=kOutput, calls=%fused_computation.2 | convolution fusion | flops 3228041216 | bytes 8685568 | tf_op jit(solution)/shard_map/dot_general | solution.py:22
  43.8 0.0 all-reduce.3.cloned.1.call-update
  43.8 111.3 %all-reduce.3.cloned.1.call-done = (f32[128,512]{1,0:T(8,128)}, f32[128,512]{1,0:T(8,128)}) async-done(((f32[128,512]{1,0:T(8,128)}, f32[128,512]{1,0:T(8,128)}), (f32[128,512]{1,0:T(8,128)}, f32[128,512]{1,0:T(8,128)})) %all-reduce.3.cloned.1.call-update) | async-done | bytes 524304 | tf_op jit(solution)/shard_map/psum | solution.py:28
  155.1 1.1 add_divide_fusion
  156.2 0.0 copy-start
  156.2 8.0 %convolution_add_fusion = f32[4096,512]{1,0:T(8,128)} fusion(f32[4096,512]{1,0:T(8,128)} %param.3, f32[128,512]{1,0:T(8,128)S(1)} %add_divide_fusion, s32[4096]{0:T(1024)S(1)} %copy-done.1), kind=kOutput, calls=%fused_computation.9 | convolution fusion | flops 3223846912 | bytes 17055744 | tf_op jit(solution)/shard_map/dot_general | solution.py:30
  164.2 0.0 copy-done
  (1 shorter events, 0.0 us)
Async XLA Ops:
  7.2 147.9 %all-reduce.3.cloned.1.call-start = ((), (), s32[]{:S(2)}) async-start(), calls=%async_computation | async-start | bytes 1048576 | tf_op jit(solution)/shard_map/psum | solution.py:28
  22.8 5.8 %copy-start.1 = (s32[4096]{0:T(1024)S(1)}, s32[4096]{0:T(1024)}, u32[]{:S(2)}) copy-start(s32[4096]{0:T(1024)} %param.4) | copy-start | bytes 49156
  28.6 7.2 %copy-start.2 = (s32[4096]{0:T(1024)S(1)}, s32[4096]{0:T(1024)}, u32[]{:S(2)}) copy-start(s32[4096]{0:T(1024)} %param.5) | copy-start | bytes 49156
  156.2 8.0 %copy-start = (f32[128,512]{1,0:T(8,128)}, f32[128,512]{1,0:T(8,128)S(1)}, u32[]{:S(2)}) copy-start(f32[128,512]{1,0:T(8,128)S(1)} %add_divide_fusion) | copy-start | bytes 786436
Sparse Core Ops, SparseCore 0:
  43.9 111.1 all-reduce.2
where the time goes:
time: 171 us
  waiting for transfers between devices  111 us (65%)
  matrix products  23.1 us (14%)
  other arithmetic  15.4 us (9%)
  between operations  14.1 us (8%)
  blocking collectives  7.01 us (4%)
    psum x1, waiting for transfers between devices, per_device(): g_sum, h_sum = lax.psum((g_part, h_part), 'rows')  111 us
    dot_general x1, matrix products, per_device(): lax.dot_general(onehot, grad, dims, precision=lax.Precision.HIGHEST, pref...  7.99 us
    dot_general x1, matrix products, per_device(): jnp.dot(onehot, leaf_values, precision=lax.Precision.HIGHEST, preferred_e...  7.98 us
    dot_general x1, matrix products, per_device(): lax.dot_general(onehot, hess, dims, precision=lax.Precision.HIGHEST, pref...  7.15 us
    div x1, other arithmetic, per_device(): prob = expo / total  5.76 us
    reduce_sum x1, other arithmetic, per_device(): total = lax.psum(jnp.sum(expo, axis=1, keepdims=True), 'cls')  4.59 us
    reduce_max x1, other arithmetic, per_device(): peak = lax.pmax(jnp.max(logits, axis=1, keepdims=True), 'cls')  4 us
    pmax x1, blocking collectives, per_device(): peak = lax.pmax(jnp.max(logits, axis=1, keepdims=True), 'cls')  3.64 us
  transfers between devices with their start and end apart: 1, of which 1 were waited for; matrix products, arithmetic and copies ran while one was open for 0% of the time, Pallas kernels for 0%

commit v1 on v0

v1 whole, which is shorter than its diff:
```python
import functools

import jax
import jax.numpy as jnp
from jax import lax
from jax.experimental import pallas as pl
from jax.experimental.pallas import tpu as pltpu
from jax.sharding import PartitionSpec as P

LEAVES = 128
LANE = 128
MIB = 2**20
F32 = jnp.float32
BF16 = jnp.bfloat16
IN_VMEM = pl.BlockSpec(memory_space=pltpu.VMEM)
IN_SMEM = pl.BlockSpec(memory_space=pltpu.SMEM)
IN_ANY = pl.BlockSpec(memory_space=pl.ANY)


def split(value):
    high = value.astype(BF16)
    return high, (value - high.astype(F32)).astype(BF16)


def params(limit):
    return pltpu.CompilerParams(vmem_limit_bytes=limit * MIB)


def stats_body(chunks, x_hbm, x_ref, e_ref, m_ref, s_ref, sems):
    step = x_hbm.shape[0] // chunks

    def fetch(i):
        at = pl.ds(i * step, step)
        return pltpu.make_async_copy(x_hbm.at[at], x_ref.at[at], sems.at[i])

    for i in range(chunks):
        fetch(i).start()
    diagonal = lax.broadcasted_iota(jnp.int32, (LANE, LANE), 0) == lax.broadcasted_iota(jnp.int32, (LANE, LANE), 1)
    for i in range(chunks):
        fetch(i).wait()
        for t in range(step // LANE):
            row = i * (step // LANE) + t
            at = pl.ds(row * LANE, LANE)
            x = x_ref[at]
            m = jnp.max(x, axis=1, keepdims=True)
            e = jnp.exp(x - m)
            s = jnp.sum(e, axis=1, keepdims=True)
            e_ref[at] = e
            m_ref[pl.ds(row, 1)] = jnp.sum(jnp.where(diagonal, m, 0.0), axis=0, keepdims=True)
            s_ref[pl.ds(row, 1)] = jnp.sum(jnp.where(diagonal, s, 0.0), axis=0, keepdims=True)


def local_stats(logits):
    rows, width = logits.shape
    chunks = 8
    full = pltpu.VMEM((rows, width), F32)
    small = jax.ShapeDtypeStruct((rows // LANE, LANE), F32)
    return pl.pallas_call(
        functools.partial(stats_body, chunks),
        out_shape=[full, full, small, small],
        in_specs=[IN_ANY],
        out_specs=[IN_VMEM] * 4,
        scratch_shapes=[pltpu.SemaphoreType.DMA((chunks,))],
        compiler_params=params(36),
        cost_estimate=pl.CostEstimate(flops=6 * rows * width, bytes_accessed=4 * rows * width, transcendentals=rows * width),
        name="local_stats",
    )(logits)


def index_body(offset_ref, leaf_ref, label_ref, cols_ref, rows_ref, class_ref):
    offset = offset_ref[0]
    sub = lax.broadcasted_iota(jnp.int32, (LANE, LANE), 0)
    lane = lax.broadcasted_iota(jnp.int32, (LANE, LANE), 1)
    for t in range(leaf_ref.shape[0]):
        at = pl.ds(t * LANE, LANE)
        leaf = jnp.broadcast_to(leaf_ref[pl.ds(t, 1)], (LANE, LANE))
        label = jnp.broadcast_to(label_ref[pl.ds(t, 1)] - offset, (LANE, LANE))
        cols_ref[:, at] = jnp.where(sub == leaf, 1.0, 0.0).astype(BF16)
        rows_ref[at] = jnp.where(lane == leaf.T, 1.0, 0.0).astype(BF16)
        class_ref[at] = label.T


def index_forms(offset, leaf_index, labels):
    rows = leaf_index.shape[0]
    shape = (rows // LANE, LANE)
    return pl.pallas_call(
        index_body,
        out_shape=[
            pltpu.VMEM((LEAVES, rows), BF16),
            pltpu.VMEM((rows, LEAVES), BF16),
            pltpu.VMEM((rows, LANE), jnp.int32),
        ],
        in_specs=[IN_SMEM, IN_VMEM, IN_VMEM],
        out_specs=[IN_VMEM] * 3,
        compiler_params=params(4),
        name="index_forms",
    )(offset, leaf_index.reshape(shape), labels.reshape(shape))


def sums_body(first, parties, block_ref, e_ref, hot_ref, class_ref, *refs):
    if first:
        peaks, totals = refs[:parties], refs[parties : 2 * parties]
        out_ref, scale_ref, acc_ref = refs[2 * parties :]
        peak = functools.reduce(jnp.maximum, [p[...] for p in peaks])
        grown = [jnp.exp(p[...] - peak) for p in peaks]
        total = functools.reduce(jnp.add, [g * t[...] for g, t in zip(grown, totals)])
        factor = grown[0] / total
    else:
        scale_ref, out_ref, acc_ref = refs
    start = pl.multiple_of(block_ref[0] * LANE, LANE)
    columns = pl.ds(start, LANE)
    step = 512
    own = lax.broadcasted_iota(jnp.int32, (step, LANE), 1) + start
    for i in range(e_ref.shape[0] // step):
        at = pl.ds(i * step, step)
        if first:
            for t in range(step // LANE):
                row = i * (step // LANE) + t
                scale_ref[pl.ds(row * LANE, LANE)] = jnp.broadcast_to(factor[row : row + 1], (LANE, LANE)).T
        prob = e_ref[at, columns] * scale_ref[at]
        grad = jnp.where(class_ref[at] == own, prob - 1.0, prob)
        hess = prob * (1.0 - prob)
        right = jnp.concatenate(split(grad) + split(hess), axis=1)
        part = jnp.dot(hot_ref[:, at], right, preferred_element_type=F32)
        if i == 0:
            acc_ref[...] = part
        else:
            acc_ref[...] += part
    out_ref[:LEAVES] = acc_ref[:, :LANE] + acc_ref[:, LANE : 2 * LANE]
    out_ref[LEAVES:] = acc_ref[:, 2 * LANE : 3 * LANE] + acc_ref[:, 3 * LANE :]


def leaf_sums(block, e, hot, classes, scale=None, stats=None):
    rows = e.shape[0]
    first = scale is None
    out = [jax.ShapeDtypeStruct((2 * LEAVES, LANE), F32)]
    if first:
        out.append(pltpu.VMEM((rows, LANE), F32))
        more = [s[0] for s in stats] + [s[1] for s in stats]
    else:
        more = [scale]
    got = pl.pallas_call(
        functools.partial(sums_body, first, len(more) // 2),
        out_shape=out,
        in_specs=[IN_SMEM] + [IN_VMEM] * (3 + len(more)),
        out_specs=[IN_VMEM] * len(out),
        scratch_shapes=[pltpu.VMEM((LEAVES, 4 * LANE), F32)],
        compiler_params=params(6),
        cost_estimate=pl.CostEstimate(flops=8 * rows * LEAVES * LANE, bytes_accessed=8 * rows * LANE, transcendentals=0),
        name="leaf_sums",
    )(block, e, hot, classes, *more)
    return got if first else got[0]


def apply_body(first, chunks, block_ref, value_ref, x_ref, hot_ref, *refs):
    if not first:
        refs = refs[2:]
    value_hbm, updated_hbm, tile_ref, sems = refs
    columns = pl.ds(pl.multiple_of(block_ref[0] * LANE, LANE), LANE)
    step = x_ref.shape[0] // chunks

    def send(i):
        at = pl.ds(i * step, step)
        return pltpu.make_async_copy(tile_ref.at[at], updated_hbm.at[at, columns], sems.at[i])

    value_copy = pltpu.make_async_copy(value_ref, value_hbm.at[:, columns], sems.at[chunks])
    value_copy.start()
    right = jnp.concatenate(split(value_ref[...]), axis=0)
    for i in range(chunks):
        at = pl.ds(i * step, step)
        hot = hot_ref[at]
        left = jnp.concatenate([hot, hot], axis=1)
        tile_ref[at] = x_ref[at, columns] + jnp.dot(left, right, preferred_element_type=F32)
        send(i).start()
    for i in range(chunks):
        send(i).wait()
    value_copy.wait()


def apply_block(block, value, x, hot, held=None):
    rows, width = x.shape
    chunks = 8
    first = held is None
    more = [] if first else list(held)
    return pl.pallas_call(
        functools.partial(apply_body, first, chunks),
        out_shape=[jax.ShapeDtypeStruct((LEAVES, width), F32), jax.ShapeDtypeStruct((rows, width), F32)],
        in_specs=[IN_SMEM] + [IN_VMEM] * 3 + [IN_ANY] * len(more),
        out_specs=[IN_ANY] * 2,
        scratch_shapes=[pltpu.VMEM((rows, LANE), F32), pltpu.SemaphoreType.DMA((chunks + 1,))],
        input_output_aliases={} if first else {4: 0, 5: 1},
        compiler_params=params(6),
        cost_estimate=pl.CostEstimate(flops=4 * rows * LEAVES * LANE, bytes_accessed=8 * rows * LANE, transcendentals=0),
        name="apply_block",
    )(block, value, x, hot, *more)


def newton(sums):
    return -0.3 * sums[:LEAVES] / (sums[LEAVES:] + 1.0)


def per_device(n_rows, n_cls, logits, leaf_index, labels):
    width = logits.shape[1]
    blocks = width // LANE
    me = lax.axis_index("rows").astype(jnp.int32)
    offset = (lax.axis_index("cls") * width).astype(jnp.int32).reshape(1)

    def swap(value, bit):
        return lax.ppermute(value, "rows", [(i, i ^ bit) for i in range(n_rows)])

    x, e, peak, total = local_stats(logits)
    mine = jnp.stack([peak, total])
    stats = [mine]
    for shift in range(1, n_cls):
        stats.append(lax.ppermute(mine, "cls", [(i, (i + shift) % n_cls) for i in range(n_cls)]))
    hot_cols, hot_rows, classes = index_forms(offset, leaf_index, labels)

    planes = n_rows == 16 and blocks == 4
    order = [1, 3, 2, 0] if planes else list(range(blocks))
    where = [((me & 3) ^ d).reshape(1) if planes else jnp.full((1,), d, jnp.int32) for d in order]
    scale = None
    parts = []
    for block in where:
        if scale is None:
            part, scale = leaf_sums(block, e, hot_cols, classes, stats=stats)
        else:
            part = leaf_sums(block, e, hot_cols, classes, scale=scale)
        parts.append(part)

    if planes:
        got = [swap(part, d) for part, d in zip(parts[:3], order[:3])]
        sums = parts[3] + got[0] + got[1] + got[2]
        sums = sums + swap(sums, 4)
        sums = sums + swap(sums, 8)
        value = newton(sums)
        values = [(where[3], value)] + [(w, swap(value, d)) for w, d in zip(where[:3], order[:3])]
    else:
        values = list(zip(where, [newton(s) for s in lax.psum(parts, "rows")]))

    held = None
    for block, value in values:
        held = apply_block(block, value, x, hot_rows, held)
    return held[0], held[1]


def solution(mesh):
    return jax.shard_map(
        functools.partial(per_device, mesh.shape["rows"], mesh.shape["cls"]),
        mesh=mesh,
        in_specs=(P("rows", "cls"), P("rows"), P("rows")),
        out_specs=(P(None, "cls"), P("rows", "cls")),
        check_vma=False,
    )
```

time: 171 us -> 53.5 us (0.31)
  waiting for transfers between devices: 111 us -> 13.1 us
  matrix products: 23.1 us -> 0 us
  Pallas kernels: 0 us -> 16.5 us
  other arithmetic: 15.4 us -> 0.08 us
  between operations: 14.1 us -> 0.81 us
  starting transfers between devices: 0.04 us -> 12.8 us
  local copies, waits for them, and re-layouts: 0.02 us -> 10 us
  blocking collectives: 7.01 us -> 0 us
    psum x1 -> x0, waiting for transfers between devices: 111 us -> none  [per_device(): g_sum, h_sum = lax.psum((g_part, h_part), 'rows')]
    dot_general x3 -> x0, matrix products: 23.1 us -> none  [the longest x1 7.99 us: per_device(): lax.dot_general(onehot, grad, dims, precision=lax.Precision.HIGHEST, pref...]
    pallas_call x0 -> x10, Pallas kernels: none -> 16.5 us  [the longest x4 6.92 us: apply_block(): pl.pallas_call(functools.partial(apply_body, first, chunks), out_shape=[j...]
    ppermute x0 -> x9, waiting for transfers between devices: none -> 13.1 us  [the longest x8 13.1 us: swap(): return lax.ppermute(value, 'rows', [(i, i ^ bit) for i in range(n_rows)])]
    ppermute x0 -> x9, starting transfers between devices: none -> 12.8 us  [the longest x8 12.4 us: swap(): return lax.ppermute(value, 'rows', [(i, i ^ bit) for i in range(n_rows)])]
    unnamed x6 -> x14, local copies, waits for them, and re-layouts: 0.02 us -> 10 us
    div x2 -> x1, other arithmetic: 6.84 us -> 0.02 us  [newton(): return -0.3 * sums[:LEAVES] / (sums[LEAVES:] + 1.0)]
    reduce_sum x1 -> x0, other arithmetic: 4.59 us -> none  [per_device(): total = lax.psum(jnp.sum(expo, axis=1, keepdims=True), 'cls')]
  transfers between devices with their start and end apart: 1 -> 9, of which waited for: 1 -> 5; matrix products, arithmetic and copies ran while one was open for 0% -> 0% of each run, Pallas kernels for 0% -> 16%
where the time goes in v1:
time: 53.5 us; the launch traced here: 53.3 us
  Pallas kernels  16.5 us (31%)
  waiting for transfers between devices  13.1 us (24%)
  starting transfers between devices  12.8 us (24%)
  local copies, waits for them, and re-layouts  10 us (19%)
  between operations  0.81 us (2%)
    ppermute x8, waiting for transfers between devices, swap(): return lax.ppermute(value, 'rows', [(i, i ^ bit) for i in range(n_rows)])  13.1 us
    ppermute x8, starting transfers between devices, swap(): return lax.ppermute(value, 'rows', [(i, i ^ bit) for i in range(n_rows)])  12.4 us
    unnamed x14, local copies, waits for them, and re-layouts  10 us
    pallas_call x4, Pallas kernels, apply_block(): pl.pallas_call(functools.partial(apply_body, first, chunks), out_shape=[j...  6.92 us
    pallas_call x4, Pallas kernels, leaf_sums(): pl.pallas_call(functools.partial(sums_body, first, len(more) // 2), out_s...  4.48 us
    pallas_call x1, Pallas kernels, local_stats(): pl.pallas_call(functools.partial(stats_body, chunks), out_shape=[full, fu...  3.88 us
    pallas_call x1, Pallas kernels, index_forms(): pl.pallas_call(index_body, out_shape=[pltpu.VMEM((LEAVES, rows), BF16), p...  1.18 us
  transfers between devices with their start and end apart: 9, of which 5 were waited for; matrix products, arithmetic and copies ran while one was open for 0% of the time, Pallas kernels for 16%

profile of v1, /device:TPU:0, one launch (start us, length us, event | category | flops | bytes accessed | tf_op | source)
XLA Modules:
  0.0 53.3 jit_solution(6097345832208554918)
XLA Ops:
  0.6 3.9 %local_stats.1 = (f32[4096,512]{1,0:T(8,128)S(1)}, f32[4096,512]{1,0:T(8,128)S(1)}, f32[32,128]{1,0:T(8,128)S(1)}, f32[32,128]{1,0:T(8,128)S(1)}) custom-call(f32[4096,512]{1,0:T(8,128)} %x_hbm.1), custom_call_target="tpu_custom_call" | custom-call | flops 12582912 | bytes 8388608 | tf_op jit(solution)/shard_map/local_stats/pallas_call | solution.py:58
  4.5 0.0 copy-start
  4.5 3.4 %copy-done = f32[4096,512]{1,0:T(8,128)} copy-done((f32[4096,512]{1,0:T(8,128)}, f32[4096,512]{1,0:T(8,128)S(1)}, u32[]{:S(2)}) %copy-start) | copy-done | bytes 8388632
  7.9 3.2 %copy-done.2 = f32[4096,512]{1,0:T(8,128)} copy-done((f32[4096,512]{1,0:T(8,128)}, f32[4096,512]{1,0:T(8,128)S(1)}, u32[]{:S(2)}) %copy-start.2) | copy-done | bytes 8388632
  11.2 0.5 collective-permute-start
  11.6 1.2 %index_forms.1 = (bf16[128,4096]{1,0:T(8,128)(2,1)S(1)}, bf16[4096,128]{1,0:T(8,128)(2,1)S(1)}, s32[4096,128]{1,0:T(8,128)S(1)}) custom-call(s32[1]{0:T(128)} %bitcast.2.offset_ref, s32[32,128]{1,0:T(8,128)S(1)} %bitcast.17, s32[32,128]{1,0:T(8,128)S(1)} %bitcast.18), custom_call_target="tpu_custom_call" | custom-call | tf_op jit(solution)/shard_map/index_forms/pallas_call | solution.py:86
  12.8 0.0 collective-permute-done
  12.9 0.0 copy-start.1
  12.9 3.4 %copy-done.1 = f32[4096,512]{1,0:T(8,128)S(1)} copy-done((f32[4096,512]{1,0:T(8,128)S(1)}, f32[4096,512]{1,0:T(8,128)}, u32[]{:S(2)}) %copy-start.1) | copy-done | bytes 8388632
  16.2 1.1 %leaf_sums.4 = (f32[256,128]{1,0:T(8,128)S(1)}, f32[4096,128]{1,0:T(8,128)S(1)}) custom-call(s32[1]{0:T(128)} %bitcast.5.block_ref, f32[4096,512]{1,0:T(8,128)S(1)} %copy-done.1, bf16[128,4096]{1,0:T(8,128)(2,1)S(1)} %get-tuple-element.18.hot_ref, s32[4096,128]{1,0:T(8,128)S(1)} %get-tuple-element.19.class_ref, f32[32,128]{1,0:T(8,128)S(1)} %get-tuple-element.20.refs_0_, ...), custom_call_target="tpu_custom_call" | custom-call | flops 536870912 | bytes 4194304 | tf_op jit(solution)/shard_map/leaf_sums/pallas_call | solution.py:142
  17.4 1.2 %leaf_sums.6 = f32[256,128]{1,0:T(8,128)S(1)} custom-call(s32[1]{0:T(128)} %bitcast.10.block_ref, f32[4096,512]{1,0:T(8,128)S(1)} %copy-done.1, bf16[128,4096]{1,0:T(8,128)(2,1)S(1)} %get-tuple-element.18.hot_ref, s32[4096,128]{1,0:T(8,128)S(1)} %get-tuple-element.19.class_ref, f32[4096,128]{1,0:T(8,128)S(1)} %get-tuple-element.22.refs_0_), custom_call_target="tpu_custom_call" | custom-call | flops 536870912 | bytes 4194304 | tf_op jit(solution)/shard_map/leaf_sums/pallas_call | solution.py:142
  18.6 3.5 %collective-permute-start.2 = (f32[256,128]{1,0:T(8,128)S(1)}, f32[256,128]{1,0:T(8,128)S(1)}, u32[]{:S(2)}, u32[]{:S(2)}) collective-permute-start(f32[256,128]{1,0:T(8,128)S(1)} %leaf_sums.6), channel_id=1, source_target_pairs={{0,6},{2,4},{4,2},{6,0},{8,14},{10,12},{12,10},{14,8},{16,22},{18,... | collective-permute-start | bytes 393224 | tf_op jit(solution)/shard_map/ppermute | solution.py:209
  22.0 1.1 %leaf_sums.7 = f32[256,128]{1,0:T(8,128)S(1)} custom-call(s32[1]{0:T(128)} %bitcast.block_ref, f32[4096,512]{1,0:T(8,128)S(1)} %copy-done.1, bf16[128,4096]{1,0:T(8,128)(2,1)S(1)} %get-tuple-element.18.hot_ref, s32[4096,128]{1,0:T(8,128)S(1)} %get-tuple-element.19.class_ref, f32[4096,128]{1,0:T(8,128)S(1)} %get-tuple-element.22.refs_0_), custom_call_target="tpu_custom_call" | custom-call | flops 536870912 | bytes 4194304 | tf_op jit(solution)/shard_map/leaf_sums/pallas_call | solution.py:142
  23.1 0.0 slice-start
  23.1 0.6 %collective-permute-start.3 = (f32[256,128]{1,0:T(8,128)S(1)}, f32[256,128]{1,0:T(8,128)S(1)}, u32[]{:S(2)}, u32[]{:S(2)}) collective-permute-start(f32[256,128]{1,0:T(8,128)S(1)} %leaf_sums.7), channel_id=1, source_target_pairs={{0,4},{2,6},{4,0},{6,2},{8,12},{10,14},{12,8},{14,10},{16,20},{18,... | collective-permute-start | bytes 393224 | tf_op jit(solution)/shard_map/ppermute | solution.py:209
  23.8 0.1 collective-permute-start.1
  23.9 1.1 %leaf_sums.5 = f32[256,128]{1,0:T(8,128)S(1)} custom-call(s32[1]{0:T(128)} %bitcast.1.block_ref, f32[4096,512]{1,0:T(8,128)S(1)} %copy-done.1, bf16[128,4096]{1,0:T(8,128)(2,1)S(1)} %get-tuple-element.18.hot_ref, s32[4096,128]{1,0:T(8,128)S(1)} %get-tuple-element.19.class_ref, f32[4096,128]{1,0:T(8,128)S(1)} %get-tuple-element.22.refs_0_), custom_call_target="tpu_custom_call" | custom-call | flops 536870912 | bytes 4194304 | tf_op jit(solution)/shard_map/leaf_sums/pallas_call | solution.py:142
  25.0 1.3 %collective-permute-done.2 = f32[256,128]{1,0:T(8,128)S(1)} collective-permute-done((f32[256,128]{1,0:T(8,128)S(1)}, f32[256,128]{1,0:T(8,128)S(1)}, u32[]{:S(2)}, u32[]{:S(2)}) %collective-permute-start.2) | collective-permute-done | bytes 131104 | tf_op jit(solution)/shard_map/ppermute | solution.py:209
  26.2 2.8 %collective-permute-done.3 = f32[256,128]{1,0:T(8,128)S(1)} collective-permute-done((f32[256,128]{1,0:T(8,128)S(1)}, f32[256,128]{1,0:T(8,128)S(1)}, u32[]{:S(2)}, u32[]{:S(2)}) %collective-permute-start.3) | collective-permute-done | bytes 131104 | tf_op jit(solution)/shard_map/ppermute | solution.py:209
  29.0 0.2 collective-permute-done.1
  29.3 1.7 %collective-permute-start.4 = (f32[256,128]{1,0:T(8,128)S(1)}, f32[256,128]{1,0:T(8,128)S(1)}, u32[]{:S(2)}, u32[]{:S(2)}) collective-permute-start(f32[256,128]{1,0:T(8,128)S(1)} %add_add_fusion), channel_id=1, source_target_pairs={{0,8},{2,10},{4,12},{6,14},{8,0},{10,2},{12,4},{14,6},{16,24},{18,... | collective-permute-start | bytes 393224 | tf_op jit(solution)/shard_map/ppermute | solution.py:209
  30.9 3.4 %collective-permute-done.4 = f32[256,128]{1,0:T(8,128)S(1)} collective-permute-done((f32[256,128]{1,0:T(8,128)S(1)}, f32[256,128]{1,0:T(8,128)S(1)}, u32[]{:S(2)}, u32[]{:S(2)}) %collective-permute-start.4) | collective-permute-done | bytes 131104 | tf_op jit(solution)/shard_map/ppermute | solution.py:209
  34.4 2.8 %collective-permute-start.5 = (f32[256,128]{1,0:T(8,128)S(1)}, f32[256,128]{1,0:T(8,128)S(1)}, u32[]{:S(2)}, u32[]{:S(2)}) collective-permute-start(f32[256,128]{1,0:T(8,128)S(1)} %add.24), channel_id=1, source_target_pairs={{0,16},{2,18},{4,20},{6,22},{8,24},{10,26},{12,28},{14,30},{16,0},... | collective-permute-start | bytes 393224 | tf_op jit(solution)/shard_map/ppermute | solution.py:209
  37.2 5.4 %collective-permute-done.5 = f32[256,128]{1,0:T(8,128)S(1)} collective-permute-done((f32[256,128]{1,0:T(8,128)S(1)}, f32[256,128]{1,0:T(8,128)S(1)}, u32[]{:S(2)}, u32[]{:S(2)}) %collective-permute-start.5) | collective-permute-done | bytes 131104 | tf_op jit(solution)/shard_map/ppermute | solution.py:209
  42.6 2.0 %collective-permute-start.8 = (f32[128,128]{1,0:T(8,128)S(1)}, f32[128,128]{1,0:T(8,128)S(1)}, u32[]{:S(2)}, u32[]{:S(2)}) collective-permute-start(f32[128,128]{1,0:T(8,128)S(1)} %fusion.value_ref), channel_id=1, source_target_pairs={{0,2},{2,0},{4,6},{6,4},{8,10},{10,8},{12,14},{14,12},{16,18},{18,... | collective-permute-start | bytes 196616 | tf_op jit(solution)/shard_map/ppermute | solution.py:209
  44.6 1.5 %collective-permute-start.7 = (f32[128,128]{1,0:T(8,128)S(1)}, f32[128,128]{1,0:T(8,128)S(1)}, u32[]{:S(2)}, u32[]{:S(2)}) collective-permute-start(f32[128,128]{1,0:T(8,128)S(1)} %fusion.value_ref), channel_id=1, source_target_pairs={{0,6},{2,4},{4,2},{6,0},{8,14},{10,12},{12,10},{14,8},{16,22},{18,... | collective-permute-start | bytes 196616 | tf_op jit(solution)/shard_map/ppermute | solution.py:209
  46.2 0.1 collective-permute-start.6
  46.3 1.7 %apply_block.4 = (f32[128,512]{1,0:T(8,128)}, f32[4096,512]{1,0:T(8,128)}) custom-call(s32[1]{0:T(128)} %bitcast.1.block_ref, f32[128,128]{1,0:T(8,128)S(1)} %fusion.value_ref, f32[4096,512]{1,0:T(8,128)S(1)} %bitcast.14, bf16[4096,128]{1,0:T(8,128)(2,1)S(1)} %get-tuple-element.25.hot_ref), custom_call_target="tpu_custom_call" | custom-call | flops 268435456 | bytes 4194304 | tf_op jit(solution)/shard_map/apply_block/pallas_call | solution.py:185
  48.1 1.7 %apply_block.5 = (f32[128,512]{1,0:T(8,128)}, f32[4096,512]{1,0:T(8,128)}) custom-call(s32[1]{0:T(128)} %bitcast.5.block_ref, f32[128,128]{1,0:T(8,128)S(1)} %collective-permute-done.8.value_ref, f32[4096,512]{1,0:T(8,128)S(1)} %bitcast.14, bf16[4096,128]{1,0:T(8,128)(2,1)S(1)} %get-tuple-element.25.hot_ref, ...), custom_call_target="tpu_custom_call", output_to_operand_aliasing={{0}: (4, {}), {1}: (5, {})} | custom-call | flops 268435456 | bytes 4194304 | tf_op jit(solution)/shard_map/apply_block/pallas_call | solution.py:185
  49.8 1.7 %apply_block.6 = (f32[128,512]{1,0:T(8,128)}, f32[4096,512]{1,0:T(8,128)}) custom-call(s32[1]{0:T(128)} %bitcast.10.block_ref, f32[128,128]{1,0:T(8,128)S(1)} %collective-permute-done.7.value_ref, f32[4096,512]{1,0:T(8,128)S(1)} %bitcast.14, bf16[4096,128]{1,0:T(8,128)(2,1)S(1)} %get-tuple-element.25.hot_ref, ...), custom_call_target="tpu_custom_call", output_to_operand_aliasing={{0}: (4, {}), {1}: (5, {})} | custom-call | flops 268435456 | bytes 4194304 | tf_op jit(solution)/shard_map/apply_block/pallas_call | solution.py:185
  51.6 0.0 collective-permute-done.6.value_ref
  51.6 1.7 %apply_block.7 = (f32[128,512]{1,0:T(8,128)}, f32[4096,512]{1,0:T(8,128)}) custom-call(s32[1]{0:T(128)} %bitcast.block_ref, f32[128,128]{1,0:T(8,128)S(1)} %collective-permute-done.6.value_ref, f32[4096,512]{1,0:T(8,128)S(1)} %bitcast.14, bf16[4096,128]{1,0:T(8,128)(2,1)S(1)} %get-tuple-element.25.hot_ref, ...), custom_call_target="tpu_custom_call", output_to_operand_aliasing={{0}: (4, {}), {1}: (5, {})} | custom-call | flops 268435456 | bytes 4194304 | tf_op jit(solution)/shard_map/apply_block/pallas_call | solution.py:185
  (17 shorter events, 0.1 us)
Async XLA Ops:
  0.6 11.0 %copy-start.3 = (s32[4096]{0:T(1024)S(1)}, s32[4096]{0:T(1024)}, u32[]{:S(2)}) copy-start(s32[4096]{0:T(1024)} %param.4) | copy-start | bytes 49156
  0.6 11.0 %copy-start.4 = (s32[4096]{0:T(1024)S(1)}, s32[4096]{0:T(1024)}, u32[]{:S(2)}) copy-start(s32[4096]{0:T(1024)} %param.5) | copy-start | bytes 49156
  4.5 3.4 %copy-start = (f32[4096,512]{1,0:T(8,128)}, f32[4096,512]{1,0:T(8,128)S(1)}, u32[]{:S(2)}) copy-start(f32[4096,512]{1,0:T(8,128)S(1)} %get-tuple-element.17.e_ref) | copy-start | bytes 25165828
  7.9 3.2 %copy-start.2 = (f32[4096,512]{1,0:T(8,128)}, f32[4096,512]{1,0:T(8,128)S(1)}, u32[]{:S(2)}) copy-start(f32[4096,512]{1,0:T(8,128)S(1)} %get-tuple-element.24.x_ref) | copy-start | bytes 25165828
  11.2 1.6 %collective-permute-start = (f32[2,32,128]{2,1,0:T(8,128)S(1)}, f32[2,32,128]{2,1,0:T(8,128)S(1)}, u32[]{:S(2)}, u32[]{:S(2)}) collective-permute-start(f32[2,32,128]{2,1,0:T(8,128)S(1)} %pad_maximum_fusion), channel_id=1, source_target_pairs={{0,1},{1,0},{2,3},{3,2},{4,5},{5,4},{6,7},{7,6},{8,9},{9,8},{10,11... | collective-permute-start | bytes 98312 | tf_op jit(solution)/shard_map/ppermute | solution.py:215
  12.9 3.4 %copy-start.1 = (f32[4096,512]{1,0:T(8,128)S(1)}, f32[4096,512]{1,0:T(8,128)}, u32[]{:S(2)}) copy-start(f32[4096,512]{1,0:T(8,128)} %copy-done) | copy-start | bytes 25165828
  18.6 7.7 %collective-permute-start.2 = (f32[256,128]{1,0:T(8,128)S(1)}, f32[256,128]{1,0:T(8,128)S(1)}, u32[]{:S(2)}, u32[]{:S(2)}) collective-permute-start(f32[256,128]{1,0:T(8,128)S(1)} %leaf_sums.6), channel_id=1, source_target_pairs={{0,6},{2,4},{4,2},{6,0},{8,14},{10,12},{12,10},{14,8},{16,22},{18,... | collective-permute-start | bytes 393224 | tf_op jit(solution)/shard_map/ppermute | solution.py:209
  23.1 23.2 %slice-start = ((s8[8388608]{0:T(1024)(128)(4,1)}), s8[4194304]{0:T(1024)(128)(4,1)S(1)}, s32[]{:S(2)}) async-start(s8[8388608]{0:T(1024)(128)(4,1)} %bitcast.13), calls=%async_computation | async-start | bytes 8388608
  23.1 5.9 %collective-permute-start.3 = (f32[256,128]{1,0:T(8,128)S(1)}, f32[256,128]{1,0:T(8,128)S(1)}, u32[]{:S(2)}, u32[]{:S(2)}) collective-permute-start(f32[256,128]{1,0:T(8,128)S(1)} %leaf_sums.7), channel_id=1, source_target_pairs={{0,4},{2,6},{4,0},{6,2},{8,12},{10,14},{12,8},{14,10},{16,20},{18,... | collective-permute-start | bytes 393224 | tf_op jit(solution)/shard_map/ppermute | solution.py:209
  23.8 5.5 %collective-permute-start.1 = (f32[256,128]{1,0:T(8,128)S(1)}, f32[256,128]{1,0:T(8,128)S(1)}, u32[]{:S(2)}, u32[]{:S(2)}) collective-permute-start(f32[256,128]{1,0:T(8,128)S(1)} %get-tuple-element.23), channel_id=1, source_target_pairs={{0,2},{2,0},{4,6},{6,4},{8,10},{10,8},{12,14},{14,12},{16,18},{18,... | collective-permute-start | bytes 393224 | tf_op jit(solution)/shard_map/ppermute | solution.py:209
  23.9 22.5 %slice-start.1 = ((s8[8388608]{0:T(1024)(128)(4,1)}), s8[4194304]{0:T(1024)(128)(4,1)S(1)}, s32[]{:S(2)}) async-start(s8[8388608]{0:T(1024)(128)(4,1)} %bitcast.13), calls=%async_computation.1 | async-start | bytes 8388608
  29.3 5.1 %collective-permute-start.4 = (f32[256,128]{1,0:T(8,128)S(1)}, f32[256,128]{1,0:T(8,128)S(1)}, u32[]{:S(2)}, u32[]{:S(2)}) collective-permute-start(f32[256,128]{1,0:T(8,128)S(1)} %add_add_fusion), channel_id=1, source_target_pairs={{0,8},{2,10},{4,12},{6,14},{8,0},{10,2},{12,4},{14,6},{16,24},{18,... | collective-permute-start | bytes 393224 | tf_op jit(solution)/shard_map/ppermute | solution.py:209
  34.4 8.2 %collective-permute-start.5 = (f32[256,128]{1,0:T(8,128)S(1)}, f32[256,128]{1,0:T(8,128)S(1)}, u32[]{:S(2)}, u32[]{:S(2)}) collective-permute-start(f32[256,128]{1,0:T(8,128)S(1)} %add.24), channel_id=1, source_target_pairs={{0,16},{2,18},{4,20},{6,22},{8,24},{10,26},{12,28},{14,30},{16,0},... | collective-permute-start | bytes 393224 | tf_op jit(solution)/shard_map/ppermute | solution.py:209
  42.6 5.5 %collective-permute-start.8 = (f32[128,128]{1,0:T(8,128)S(1)}, f32[128,128]{1,0:T(8,128)S(1)}, u32[]{:S(2)}, u32[]{:S(2)}) collective-permute-start(f32[128,128]{1,0:T(8,128)S(1)} %fusion.value_ref), channel_id=1, source_target_pairs={{0,2},{2,0},{4,6},{6,4},{8,10},{10,8},{12,14},{14,12},{16,18},{18,... | collective-permute-start | bytes 196616 | tf_op jit(solution)/shard_map/ppermute | solution.py:209
  44.6 5.2 %collective-permute-start.7 = (f32[128,128]{1,0:T(8,128)S(1)}, f32[128,128]{1,0:T(8,128)S(1)}, u32[]{:S(2)}, u32[]{:S(2)}) collective-permute-start(f32[128,128]{1,0:T(8,128)S(1)} %fusion.value_ref), channel_id=1, source_target_pairs={{0,6},{2,4},{4,2},{6,0},{8,14},{10,12},{12,10},{14,8},{16,22},{18,... | collective-permute-start | bytes 196616 | tf_op jit(solution)/shard_map/ppermute | solution.py:209
  46.2 5.4 %collective-permute-start.6 = (f32[128,128]{1,0:T(8,128)S(1)}, f32[128,128]{1,0:T(8,128)S(1)}, u32[]{:S(2)}, u32[]{:S(2)}) collective-permute-start(f32[128,128]{1,0:T(8,128)S(1)} %fusion.value_ref), channel_id=1, source_target_pairs={{0,4},{2,6},{4,0},{6,2},{8,12},{10,14},{12,8},{14,10},{16,20},{18,... | collective-permute-start | bytes 196616 | tf_op jit(solution)/shard_map/ppermute | solution.py:209

commit v2 on v1

--- a/solution.py
+++ b/solution.py
@@ -13,7 +13,6 @@
 F32 = jnp.float32
 BF16 = jnp.bfloat16
 IN_VMEM = pl.BlockSpec(memory_space=pltpu.VMEM)
-IN_SMEM = pl.BlockSpec(memory_space=pltpu.SMEM)
 IN_ANY = pl.BlockSpec(memory_space=pl.ANY)
 
 
@@ -67,8 +66,8 @@
     )(logits)
 
 
-def index_body(offset_ref, leaf_ref, label_ref, cols_ref, rows_ref, class_ref):
-    offset = offset_ref[0]
+def index_body(width, leaf_ref, label_ref, cols_ref, rows_ref, class_ref):
+    offset = lax.axis_index("cls") * width
     sub = lax.broadcasted_iota(jnp.int32, (LANE, LANE), 0)
     lane = lax.broadcasted_iota(jnp.int32, (LANE, LANE), 1)
     for t in range(leaf_ref.shape[0]):
@@ -80,24 +79,31 @@
         class_ref[at] = label.T
 
 
-def index_forms(offset, leaf_index, labels):
+def index_forms(width, leaf_index, labels):
     rows = leaf_index.shape[0]
     shape = (rows // LANE, LANE)
     return pl.pallas_call(
-        index_body,
+        functools.partial(index_body, width),
         out_shape=[
             pltpu.VMEM((LEAVES, rows), BF16),
             pltpu.VMEM((rows, LEAVES), BF16),
             pltpu.VMEM((rows, LANE), jnp.int32),
         ],
-        in_specs=[IN_SMEM, IN_VMEM, IN_VMEM],
+        in_specs=[IN_VMEM, IN_VMEM],
         out_specs=[IN_VMEM] * 3,
         compiler_params=params(4),
         name="index_forms",
-    )(offset, leaf_index.reshape(shape), labels.reshape(shape))
-
-
-def sums_body(first, parties, block_ref, e_ref, hot_ref, class_ref, *refs):
+    )(leaf_index.reshape(shape), labels.reshape(shape))
+
+
+def block_start(planes, block):
+    if planes:
+        block = (lax.axis_index("rows") & 3) ^ block
+        return pl.multiple_of(block * LANE, LANE)
+    return block * LANE
+
+
+def sums_body(first, parties, place, e_ref, hot_ref, class_ref, *refs):
     if first:
         peaks, totals = refs[:parties], refs[parties : 2 * parties]
         out_ref, scale_ref, acc_ref = refs[2 * parties :]
@@ -107,7 +113,7 @@
         factor = grown[0] / total
     else:
         scale_ref, out_ref, acc_ref = refs
-    start = pl.multiple_of(block_ref[0] * LANE, LANE)
+    start = block_start(*place)
     columns = pl.ds(start, LANE)
     step = 512
     own = lax.broadcasted_iota(jnp.int32, (step, LANE), 1) + start
@@ -130,7 +136,7 @@
     out_ref[LEAVES:] = acc_ref[:, 2 * LANE : 3 * LANE] + acc_ref[:, 3 * LANE :]
 
 
-def leaf_sums(block, e, hot, classes, scale=None, stats=None):
+def leaf_sums(place, e, hot, classes, scale=None, stats=None):
     rows = e.shape[0]
     first = scale is None
     out = [jax.ShapeDtypeStruct((2 * LEAVES, LANE), F32)]
@@ -140,23 +146,23 @@
     else:
         more = [scale]
     got = pl.pallas_call(
-        functools.partial(sums_body, first, len(more) // 2),
+        functools.partial(sums_body, first, len(more) // 2, place),
         out_shape=out,
-        in_specs=[IN_SMEM] + [IN_VMEM] * (3 + len(more)),
+        in_specs=[IN_VMEM] * (3 + len(more)),
         out_specs=[IN_VMEM] * len(out),
         scratch_shapes=[pltpu.VMEM((LEAVES, 4 * LANE), F32)],
         compiler_params=params(6),
         cost_estimate=pl.CostEstimate(flops=8 * rows * LEAVES * LANE, bytes_accessed=8 * rows * LANE, transcendentals=0),
         name="leaf_sums",
-    )(block, e, hot, classes, *more)
+    )(e, hot, classes, *more)
     return got if first else got[0]
 
 
-def apply_body(first, chunks, block_ref, value_ref, x_ref, hot_ref, *refs):
+def apply_body(first, chunks, place, value_ref, x_ref, hot_ref, *refs):
     if not first:
         refs = refs[2:]
     value_hbm, updated_hbm, tile_ref, sems = refs
-    columns = pl.ds(pl.multiple_of(block_ref[0] * LANE, LANE), LANE)
+    columns = pl.ds(block_start(*place), LANE)
     step = x_ref.shape[0] // chunks
 
     def send(i):
@@ -177,22 +183,22 @@
     value_copy.wait()
 
 
-def apply_block(block, value, x, hot, held=None):
+def apply_block(place, value, x, hot, held=None):
     rows, width = x.shape
     chunks = 8
     first = held is None
     more = [] if first else list(held)
     return pl.pallas_call(
-        functools.partial(apply_body, first, chunks),
+        functools.partial(apply_body, first, chunks, place),
         out_shape=[jax.ShapeDtypeStruct((LEAVES, width), F32), jax.ShapeDtypeStruct((rows, width), F32)],
-        in_specs=[IN_SMEM] + [IN_VMEM] * 3 + [IN_ANY] * len(more),
+        in_specs=[IN_VMEM] * 3 + [IN_ANY] * len(more),
         out_specs=[IN_ANY] * 2,
         scratch_shapes=[pltpu.VMEM((rows, LANE), F32), pltpu.SemaphoreType.DMA((chunks + 1,))],
-        input_output_aliases={} if first else {4: 0, 5: 1},
+        input_output_aliases={} if first else {3: 0, 4: 1},
         compiler_params=params(6),
         cost_estimate=pl.CostEstimate(flops=4 * rows * LEAVES * LANE, bytes_accessed=8 * rows * LANE, transcendentals=0),
         name="apply_block",
-    )(block, value, x, hot, *more)
+    )(value, x, hot, *more)
 
 
 def newton(sums):
@@ -202,8 +208,6 @@
 def per_device(n_rows, n_cls, logits, leaf_index, labels):
     width = logits.shape[1]
     blocks = width // LANE
-    me = lax.axis_index("rows").astype(jnp.int32)
-    offset = (lax.axis_index("cls") * width).astype(jnp.int32).reshape(1)
 
     def swap(value, bit):
         return lax.ppermute(value, "rows", [(i, i ^ bit) for i in range(n_rows)])
@@ -213,11 +217,11 @@
     stats = [mine]
     for shift in range(1, n_cls):
         stats.append(lax.ppermute(mine, "cls", [(i, (i + shift) % n_cls) for i in range(n_cls)]))
-    hot_cols, hot_rows, classes = index_forms(offset, leaf_index, labels)
+    hot_cols, hot_rows, classes = index_forms(width, leaf_index, labels)
 
     planes = n_rows == 16 and blocks == 4
     order = [1, 3, 2, 0] if planes else list(range(blocks))
-    where = [((me & 3) ^ d).reshape(1) if planes else jnp.full((1,), d, jnp.int32) for d in order]
+    where = [(planes, d) for d in order]
     scale = None
     parts = []
     for block in where:

time: 53.5 us -> 45.2 us (0.84)
  local copies, waits for them, and re-layouts: 10 us -> 0.01 us
  waiting for transfers between devices: 13.1 us -> 14.8 us
    unnamed x14 -> x4, local copies, waits for them, and re-layouts: 10 us -> 0.01 us
    ppermute x8, waiting for transfers between devices: 13.1 us -> 14.8 us  [swap(): return lax.ppermute(value, 'rows', [(i, i ^ bit) for i in range(n_rows)])]
  transfers between devices with their start and end apart: 9 -> 9, of which waited for: 5 -> 5; matrix products, arithmetic and copies ran while one was open for 0% -> 0% of each run, Pallas kernels for 16% -> 17%
where the time goes in v2:
time: 45.2 us; the launch traced here: 45 us
  Pallas kernels  16.7 us (37%)
  waiting for transfers between devices  14.8 us (33%)
  starting transfers between devices  12.6 us (28%)
  between operations  0.79 us (2%)
    ppermute x8, waiting for transfers between devices, swap(): return lax.ppermute(value, 'rows', [(i, i ^ bit) for i in range(n_rows)])  14.8 us
    ppermute x8, starting transfers between devices, swap(): return lax.ppermute(value, 'rows', [(i, i ^ bit) for i in range(n_rows)])  12.1 us
    pallas_call x4, Pallas kernels, apply_block(): pl.pallas_call(functools.partial(apply_body, first, chunks, place), out_s...  6.93 us
    pallas_call x4, Pallas kernels, leaf_sums(): pl.pallas_call(functools.partial(sums_body, first, len(more) // 2, place)...  4.74 us
    pallas_call x1, Pallas kernels, local_stats(): pl.pallas_call(functools.partial(stats_body, chunks), out_shape=[full, fu...  3.88 us
    pallas_call x1, Pallas kernels, index_forms(): pl.pallas_call(functools.partial(index_body, width), out_shape=[pltpu.VME...  1.17 us
  transfers between devices with their start and end apart: 9, of which 5 were waited for; matrix products, arithmetic and copies ran while one was open for 0% of the time, Pallas kernels for 17%

profile of v2, /device:TPU:0, one launch (start us, length us, event | category | flops | bytes accessed | tf_op | source)
XLA Modules:
  0.0 45.0 jit_solution(1308152112234949966)
XLA Ops:
  0.6 0.0 copy-start
  0.6 0.0 copy-start.1
  0.6 3.9 %local_stats.1 = (f32[4096,512]{1,0:T(8,128)S(1)}, f32[4096,512]{1,0:T(8,128)S(1)}, f32[32,128]{1,0:T(8,128)S(1)}, f32[32,128]{1,0:T(8,128)S(1)}) custom-call(f32[4096,512]{1,0:T(8,128)} %x_hbm.1), custom_call_target="tpu_custom_call" | custom-call | flops 12582912 | bytes 8388608 | tf_op jit(solution)/shard_map/local_stats/pallas_call | solution.py:57
  4.5 0.5 %collective-permute-start = (f32[2,32,128]{2,1,0:T(8,128)S(1)}, f32[2,32,128]{2,1,0:T(8,128)S(1)}, u32[]{:S(2)}, u32[]{:S(2)}) collective-permute-start(f32[2,32,128]{2,1,0:T(8,128)S(1)} %pad_maximum_fusion), channel_id=1, source_target_pairs={{0,1},{1,0},{2,3},{3,2},{4,5},{5,4},{6,7},{7,6},{8,9},{9,8},{10,11... | collective-permute-start | bytes 98312 | tf_op jit(solution)/shard_map/ppermute | solution.py:219
  5.1 0.0 copy-done
  5.1 0.0 copy-done.1
  5.1 1.2 %index_forms.1 = (bf16[128,4096]{1,0:T(8,128)(2,1)S(1)}, bf16[4096,128]{1,0:T(8,128)(2,1)S(1)}, s32[4096,128]{1,0:T(8,128)S(1)}) custom-call(s32[32,128]{1,0:T(8,128)S(1)} %bitcast.10, s32[32,128]{1,0:T(8,128)S(1)} %bitcast.11), custom_call_target="tpu_custom_call" | custom-call | tf_op jit(solution)/shard_map/index_forms/pallas_call | solution.py:85
  6.3 0.0 collective-permute-done
  6.3 1.2 %leaf_sums.4 = (f32[256,128]{1,0:T(8,128)S(1)}, f32[4096,128]{1,0:T(8,128)S(1)}) custom-call(f32[4096,512]{1,0:T(8,128)S(1)} %get-tuple-element.17.e_ref, bf16[128,4096]{1,0:T(8,128)(2,1)S(1)} %get-tuple-element.18.hot_ref, s32[4096,128]{1,0:T(8,128)S(1)} %get-tuple-element.19.class_ref, f32[32,128]{1,0:T(8,128)S(1)} %get-tuple-element.20.refs_0_, ...), custom_call_target="tpu_custom_call" | custom-call | flops 536870912 | bytes 4194304 | tf_op jit(solution)/shard_map/leaf_sums/pallas_call | solution.py:148
  7.5 1.2 %leaf_sums.6 = f32[256,128]{1,0:T(8,128)S(1)} custom-call(f32[4096,512]{1,0:T(8,128)S(1)} %get-tuple-element.17.e_ref, bf16[128,4096]{1,0:T(8,128)(2,1)S(1)} %get-tuple-element.18.hot_ref, s32[4096,128]{1,0:T(8,128)S(1)} %get-tuple-element.19.class_ref, f32[4096,128]{1,0:T(8,128)S(1)} %get-tuple-element.22.refs_0_), custom_call_target="tpu_custom_call" | custom-call | flops 536870912 | bytes 4194304 | tf_op jit(solution)/shard_map/leaf_sums/pallas_call | solution.py:148
  8.7 1.2 %leaf_sums.7 = f32[256,128]{1,0:T(8,128)S(1)} custom-call(f32[4096,512]{1,0:T(8,128)S(1)} %get-tuple-element.17.e_ref, bf16[128,4096]{1,0:T(8,128)(2,1)S(1)} %get-tuple-element.18.hot_ref, s32[4096,128]{1,0:T(8,128)S(1)} %get-tuple-element.19.class_ref, f32[4096,128]{1,0:T(8,128)S(1)} %get-tuple-element.22.refs_0_), custom_call_target="tpu_custom_call" | custom-call | flops 536870912 | bytes 4194304 | tf_op jit(solution)/shard_map/leaf_sums/pallas_call | solution.py:148
  9.9 3.4 %collective-permute-start.2 = (f32[256,128]{1,0:T(8,128)S(1)}, f32[256,128]{1,0:T(8,128)S(1)}, u32[]{:S(2)}, u32[]{:S(2)}) collective-permute-start(f32[256,128]{1,0:T(8,128)S(1)} %leaf_sums.6), channel_id=1, source_target_pairs={{0,6},{2,4},{4,2},{6,0},{8,14},{10,12},{12,10},{14,8},{16,22},{18,... | collective-permute-start | bytes 393224 | tf_op jit(solution)/shard_map/ppermute | solution.py:213
  13.3 0.6 %collective-permute-start.3 = (f32[256,128]{1,0:T(8,128)S(1)}, f32[256,128]{1,0:T(8,128)S(1)}, u32[]{:S(2)}, u32[]{:S(2)}) collective-permute-start(f32[256,128]{1,0:T(8,128)S(1)} %leaf_sums.7), channel_id=1, source_target_pairs={{0,4},{2,6},{4,0},{6,2},{8,12},{10,14},{12,8},{14,10},{16,20},{18,... | collective-permute-start | bytes 393224 | tf_op jit(solution)/shard_map/ppermute | solution.py:213
  14.0 0.0 collective-permute-start.1
  14.0 1.1 %leaf_sums.5 = f32[256,128]{1,0:T(8,128)S(1)} custom-call(f32[4096,512]{1,0:T(8,128)S(1)} %get-tuple-element.17.e_ref, bf16[128,4096]{1,0:T(8,128)(2,1)S(1)} %get-tuple-element.18.hot_ref, s32[4096,128]{1,0:T(8,128)S(1)} %get-tuple-element.19.class_ref, f32[4096,128]{1,0:T(8,128)S(1)} %get-tuple-element.22.refs_0_), custom_call_target="tpu_custom_call" | custom-call | flops 536870912 | bytes 4194304 | tf_op jit(solution)/shard_map/leaf_sums/pallas_call | solution.py:148
  15.1 2.5 %collective-permute-done.2 = f32[256,128]{1,0:T(8,128)S(1)} collective-permute-done((f32[256,128]{1,0:T(8,128)S(1)}, f32[256,128]{1,0:T(8,128)S(1)}, u32[]{:S(2)}, u32[]{:S(2)}) %collective-permute-start.2) | collective-permute-done | bytes 131104 | tf_op jit(solution)/shard_map/ppermute | solution.py:213
  17.6 2.7 %collective-permute-done.3 = f32[256,128]{1,0:T(8,128)S(1)} collective-permute-done((f32[256,128]{1,0:T(8,128)S(1)}, f32[256,128]{1,0:T(8,128)S(1)}, u32[]{:S(2)}, u32[]{:S(2)}) %collective-permute-start.3) | collective-permute-done | bytes 131104 | tf_op jit(solution)/shard_map/ppermute | solution.py:213
  20.3 0.3 collective-permute-done.1
  20.6 1.6 %collective-permute-start.4 = (f32[256,128]{1,0:T(8,128)S(1)}, f32[256,128]{1,0:T(8,128)S(1)}, u32[]{:S(2)}, u32[]{:S(2)}) collective-permute-start(f32[256,128]{1,0:T(8,128)S(1)} %add_add_fusion), channel_id=1, source_target_pairs={{0,8},{2,10},{4,12},{6,14},{8,0},{10,2},{12,4},{14,6},{16,24},{18,... | collective-permute-start | bytes 393224 | tf_op jit(solution)/shard_map/ppermute | solution.py:213
  22.3 3.7 %collective-permute-done.4 = f32[256,128]{1,0:T(8,128)S(1)} collective-permute-done((f32[256,128]{1,0:T(8,128)S(1)}, f32[256,128]{1,0:T(8,128)S(1)}, u32[]{:S(2)}, u32[]{:S(2)}) %collective-permute-start.4) | collective-permute-done | bytes 131104 | tf_op jit(solution)/shard_map/ppermute | solution.py:213
  26.0 2.8 %collective-permute-start.5 = (f32[256,128]{1,0:T(8,128)S(1)}, f32[256,128]{1,0:T(8,128)S(1)}, u32[]{:S(2)}, u32[]{:S(2)}) collective-permute-start(f32[256,128]{1,0:T(8,128)S(1)} %add.24), channel_id=1, source_target_pairs={{0,16},{2,18},{4,20},{6,22},{8,24},{10,26},{12,28},{14,30},{16,0},... | collective-permute-start | bytes 393224 | tf_op jit(solution)/shard_map/ppermute | solution.py:213
  28.8 5.6 %collective-permute-done.5 = f32[256,128]{1,0:T(8,128)S(1)} collective-permute-done((f32[256,128]{1,0:T(8,128)S(1)}, f32[256,128]{1,0:T(8,128)S(1)}, u32[]{:S(2)}, u32[]{:S(2)}) %collective-permute-start.5) | collective-permute-done | bytes 131104 | tf_op jit(solution)/shard_map/ppermute | solution.py:213
  34.5 1.6 %collective-permute-start.8 = (f32[128,128]{1,0:T(8,128)S(1)}, f32[128,128]{1,0:T(8,128)S(1)}, u32[]{:S(2)}, u32[]{:S(2)}) collective-permute-start(f32[128,128]{1,0:T(8,128)S(1)} %fusion.value_ref), channel_id=1, source_target_pairs={{0,2},{2,0},{4,6},{6,4},{8,10},{10,8},{12,14},{14,12},{16,18},{18,... | collective-permute-start | bytes 196616 | tf_op jit(solution)/shard_map/ppermute | solution.py:213
  36.1 1.4 %collective-permute-start.7 = (f32[128,128]{1,0:T(8,128)S(1)}, f32[128,128]{1,0:T(8,128)S(1)}, u32[]{:S(2)}, u32[]{:S(2)}) collective-permute-start(f32[128,128]{1,0:T(8,128)S(1)} %fusion.value_ref), channel_id=1, source_target_pairs={{0,6},{2,4},{4,2},{6,0},{8,14},{10,12},{12,10},{14,8},{16,22},{18,... | collective-permute-start | bytes 196616 | tf_op jit(solution)/shard_map/ppermute | solution.py:213
  37.5 0.5 %collective-permute-start.6 = (f32[128,128]{1,0:T(8,128)S(1)}, f32[128,128]{1,0:T(8,128)S(1)}, u32[]{:S(2)}, u32[]{:S(2)}) collective-permute-start(f32[128,128]{1,0:T(8,128)S(1)} %fusion.value_ref), channel_id=1, source_target_pairs={{0,4},{2,6},{4,0},{6,2},{8,12},{10,14},{12,8},{14,10},{16,20},{18,... | collective-permute-start | bytes 196616 | tf_op jit(solution)/shard_map/ppermute | solution.py:213
  38.0 1.7 %apply_block.4 = (f32[128,512]{1,0:T(8,128)}, f32[4096,512]{1,0:T(8,128)}) custom-call(f32[128,128]{1,0:T(8,128)S(1)} %fusion.value_ref, f32[4096,512]{1,0:T(8,128)S(1)} %get-tuple-element.24.x_ref, bf16[4096,128]{1,0:T(8,128)(2,1)S(1)} %get-tuple-element.25.hot_ref), custom_call_target="tpu_custom_call" | custom-call | flops 268435456 | bytes 4194304 | tf_op jit(solution)/shard_map/apply_block/pallas_call | solution.py:191
  39.8 0.0 collective-permute-done.8.value_ref
  39.8 1.7 %apply_block.5 = (f32[128,512]{1,0:T(8,128)}, f32[4096,512]{1,0:T(8,128)}) custom-call(f32[128,128]{1,0:T(8,128)S(1)} %collective-permute-done.8.value_ref, f32[4096,512]{1,0:T(8,128)S(1)} %get-tuple-element.24.x_ref, bf16[4096,128]{1,0:T(8,128)(2,1)S(1)} %get-tuple-element.25.hot_ref, ...), custom_call_target="tpu_custom_call", output_to_operand_aliasing={{0}: (3, {}), {1}: (4, {})} | custom-call | flops 268435456 | bytes 4194304 | tf_op jit(solution)/shard_map/apply_block/pallas_call | solution.py:191
  41.5 0.0 collective-permute-done.7.value_ref
  41.5 1.7 %apply_block.6 = (f32[128,512]{1,0:T(8,128)}, f32[4096,512]{1,0:T(8,128)}) custom-call(f32[128,128]{1,0:T(8,128)S(1)} %collective-permute-done.7.value_ref, f32[4096,512]{1,0:T(8,128)S(1)} %get-tuple-element.24.x_ref, bf16[4096,128]{1,0:T(8,128)(2,1)S(1)} %get-tuple-element.25.hot_ref, ...), custom_call_target="tpu_custom_call", output_to_operand_aliasing={{0}: (3, {}), {1}: (4, {})} | custom-call | flops 268435456 | bytes 4194304 | tf_op jit(solution)/shard_map/apply_block/pallas_call | solution.py:191
  43.3 0.0 collective-permute-done.6.value_ref
  43.3 1.7 %apply_block.7 = (f32[128,512]{1,0:T(8,128)}, f32[4096,512]{1,0:T(8,128)}) custom-call(f32[128,128]{1,0:T(8,128)S(1)} %collective-permute-done.6.value_ref, f32[4096,512]{1,0:T(8,128)S(1)} %get-tuple-element.24.x_ref, bf16[4096,128]{1,0:T(8,128)(2,1)S(1)} %get-tuple-element.25.hot_ref, ...), custom_call_target="tpu_custom_call", output_to_operand_aliasing={{0}: (3, {}), {1}: (4, {})} | custom-call | flops 268435456 | bytes 4194304 | tf_op jit(solution)/shard_map/apply_block/pallas_call | solution.py:191
  (6 shorter events, 0.1 us)
Async XLA Ops:
  0.6 4.4 %copy-start = (s32[4096]{0:T(1024)S(1)}, s32[4096]{0:T(1024)}, u32[]{:S(2)}) copy-start(s32[4096]{0:T(1024)} %param.4) | copy-start | bytes 49156
  0.6 4.4 %copy-start.1 = (s32[4096]{0:T(1024)S(1)}, s32[4096]{0:T(1024)}, u32[]{:S(2)}) copy-start(s32[4096]{0:T(1024)} %param.5) | copy-start | bytes 49156
  4.5 1.7 %collective-permute-start = (f32[2,32,128]{2,1,0:T(8,128)S(1)}, f32[2,32,128]{2,1,0:T(8,128)S(1)}, u32[]{:S(2)}, u32[]{:S(2)}) collective-permute-start(f32[2,32,128]{2,1,0:T(8,128)S(1)} %pad_maximum_fusion), channel_id=1, source_target_pairs={{0,1},{1,0},{2,3},{3,2},{4,5},{5,4},{6,7},{7,6},{8,9},{9,8},{10,11... | collective-permute-start | bytes 98312 | tf_op jit(solution)/shard_map/ppermute | solution.py:219
  9.9 7.7 %collective-permute-start.2 = (f32[256,128]{1,0:T(8,128)S(1)}, f32[256,128]{1,0:T(8,128)S(1)}, u32[]{:S(2)}, u32[]{:S(2)}) collective-permute-start(f32[256,128]{1,0:T(8,128)S(1)} %leaf_sums.6), channel_id=1, source_target_pairs={{0,6},{2,4},{4,2},{6,0},{8,14},{10,12},{12,10},{14,8},{16,22},{18,... | collective-permute-start | bytes 393224 | tf_op jit(solution)/shard_map/ppermute | solution.py:213
  13.3 6.9 %collective-permute-start.3 = (f32[256,128]{1,0:T(8,128)S(1)}, f32[256,128]{1,0:T(8,128)S(1)}, u32[]{:S(2)}, u32[]{:S(2)}) collective-permute-start(f32[256,128]{1,0:T(8,128)S(1)} %leaf_sums.7), channel_id=1, source_target_pairs={{0,4},{2,6},{4,0},{6,2},{8,12},{10,14},{12,8},{14,10},{16,20},{18,... | collective-permute-start | bytes 393224 | tf_op jit(solution)/shard_map/ppermute | solution.py:213
  14.0 6.6 %collective-permute-start.1 = (f32[256,128]{1,0:T(8,128)S(1)}, f32[256,128]{1,0:T(8,128)S(1)}, u32[]{:S(2)}, u32[]{:S(2)}) collective-permute-start(f32[256,128]{1,0:T(8,128)S(1)} %get-tuple-element.23), channel_id=1, source_target_pairs={{0,2},{2,0},{4,6},{6,4},{8,10},{10,8},{12,14},{14,12},{16,18},{18,... | collective-permute-start | bytes 393224 | tf_op jit(solution)/shard_map/ppermute | solution.py:213
  20.6 5.3 %collective-permute-start.4 = (f32[256,128]{1,0:T(8,128)S(1)}, f32[256,128]{1,0:T(8,128)S(1)}, u32[]{:S(2)}, u32[]{:S(2)}) collective-permute-start(f32[256,128]{1,0:T(8,128)S(1)} %add_add_fusion), channel_id=1, source_target_pairs={{0,8},{2,10},{4,12},{6,14},{8,0},{10,2},{12,4},{14,6},{16,24},{18,... | collective-permute-start | bytes 393224 | tf_op jit(solution)/shard_map/ppermute | solution.py:213
  26.0 8.5 %collective-permute-start.5 = (f32[256,128]{1,0:T(8,128)S(1)}, f32[256,128]{1,0:T(8,128)S(1)}, u32[]{:S(2)}, u32[]{:S(2)}) collective-permute-start(f32[256,128]{1,0:T(8,128)S(1)} %add.24), channel_id=1, source_target_pairs={{0,16},{2,18},{4,20},{6,22},{8,24},{10,26},{12,28},{14,30},{16,0},... | collective-permute-start | bytes 393224 | tf_op jit(solution)/shard_map/ppermute | solution.py:213
  34.5 5.3 %collective-permute-start.8 = (f32[128,128]{1,0:T(8,128)S(1)}, f32[128,128]{1,0:T(8,128)S(1)}, u32[]{:S(2)}, u32[]{:S(2)}) collective-permute-start(f32[128,128]{1,0:T(8,128)S(1)} %fusion.value_ref), channel_id=1, source_target_pairs={{0,2},{2,0},{4,6},{6,4},{8,10},{10,8},{12,14},{14,12},{16,18},{18,... | collective-permute-start | bytes 196616 | tf_op jit(solution)/shard_map/ppermute | solution.py:213
  36.1 5.4 %collective-permute-start.7 = (f32[128,128]{1,0:T(8,128)S(1)}, f32[128,128]{1,0:T(8,128)S(1)}, u32[]{:S(2)}, u32[]{:S(2)}) collective-permute-start(f32[128,128]{1,0:T(8,128)S(1)} %fusion.value_ref), channel_id=1, source_target_pairs={{0,6},{2,4},{4,2},{6,0},{8,14},{10,12},{12,10},{14,8},{16,22},{18,... | collective-permute-start | bytes 196616 | tf_op jit(solution)/shard_map/ppermute | solution.py:213
  37.5 5.8 %collective-permute-start.6 = (f32[128,128]{1,0:T(8,128)S(1)}, f32[128,128]{1,0:T(8,128)S(1)}, u32[]{:S(2)}, u32[]{:S(2)}) collective-permute-start(f32[128,128]{1,0:T(8,128)S(1)} %fusion.value_ref), channel_id=1, source_target_pairs={{0,4},{2,6},{4,0},{6,2},{8,12},{10,14},{12,8},{14,10},{16,20},{18,... | collective-permute-start | bytes 196616 | tf_op jit(solution)/shard_map/ppermute | solution.py:213

commit v3 on v2

--- a/solution.py
+++ b/solution.py
@@ -112,7 +112,7 @@
         total = functools.reduce(jnp.add, [g * t[...] for g, t in zip(grown, totals)])
         factor = grown[0] / total
     else:
-        scale_ref, out_ref, acc_ref = refs
+        scale_ref, _, out_ref, acc_ref = refs
     start = block_start(*place)
     columns = pl.ds(start, LANE)
     step = 512
@@ -136,7 +136,7 @@
     out_ref[LEAVES:] = acc_ref[:, 2 * LANE : 3 * LANE] + acc_ref[:, 3 * LANE :]
 
 
-def leaf_sums(place, e, hot, classes, scale=None, stats=None):
+def leaf_sums(place, e, hot, classes, scale=None, stats=None, after=None):
     rows = e.shape[0]
     first = scale is None
     out = [jax.ShapeDtypeStruct((2 * LEAVES, LANE), F32)]
@@ -144,7 +144,7 @@
         out.append(pltpu.VMEM((rows, LANE), F32))
         more = [s[0] for s in stats] + [s[1] for s in stats]
     else:
-        more = [scale]
+        more = [scale, after]
     got = pl.pallas_call(
         functools.partial(sums_body, first, len(more) // 2, place),
         out_shape=out,
@@ -152,53 +152,67 @@
         out_specs=[IN_VMEM] * len(out),
         scratch_shapes=[pltpu.VMEM((LEAVES, 4 * LANE), F32)],
         compiler_params=params(6),
-        cost_estimate=pl.CostEstimate(flops=8 * rows * LEAVES * LANE, bytes_accessed=8 * rows * LANE, transcendentals=0),
+        cost_estimate=pl.CostEstimate(flops=1, bytes_accessed=1, transcendentals=0),
         name="leaf_sums",
     )(e, hot, classes, *more)
     return got if first else got[0]
 
 
-def apply_body(first, chunks, place, value_ref, x_ref, hot_ref, *refs):
+def apply_body(first, chunks, places, x_ref, hot_ref, *refs):
+    count = len(places)
+    values, refs = refs[:count], refs[count:]
     if not first:
         refs = refs[2:]
-    value_hbm, updated_hbm, tile_ref, sems = refs
-    columns = pl.ds(block_start(*place), LANE)
+    value_hbm, updated_hbm, tile_ref, sems, value_sems = refs
+    columns = [pl.ds(block_start(*place), LANE) for place in places]
     step = x_ref.shape[0] // chunks
 
-    def send(i):
-        at = pl.ds(i * step, step)
-        return pltpu.make_async_copy(tile_ref.at[at], updated_hbm.at[at, columns], sems.at[i])
-
-    value_copy = pltpu.make_async_copy(value_ref, value_hbm.at[:, columns], sems.at[chunks])
-    value_copy.start()
-    right = jnp.concatenate(split(value_ref[...]), axis=0)
+    def send(i, b):
+        at = pl.ds(i * step, step)
+        return pltpu.make_async_copy(tile_ref.at[b, at], updated_hbm.at[at, columns[b]], sems.at[i, b])
+
+    def send_value(b):
+        return pltpu.make_async_copy(values[b], value_hbm.at[:, columns[b]], value_sems.at[b])
+
+    for b in range(count):
+        send_value(b).start()
+    right = [jnp.concatenate(split(value[...]), axis=0) for value in values]
     for i in range(chunks):
         at = pl.ds(i * step, step)
         hot = hot_ref[at]
         left = jnp.concatenate([hot, hot], axis=1)
-        tile_ref[at] = x_ref[at, columns] + jnp.dot(left, right, preferred_element_type=F32)
-        send(i).start()
-    for i in range(chunks):
-        send(i).wait()
-    value_copy.wait()
-
-
-def apply_block(place, value, x, hot, held=None):
+        for b in range(count):
+            tile_ref[b, at] = x_ref[at, columns[b]] + jnp.dot(left, right[b], preferred_element_type=F32)
+            send(i, b).start()
+    for i in range(chunks):
+        for b in range(count):
+            send(i, b).wait()
+    for b in range(count):
+        send_value(b).wait()
+
+
+def apply_blocks(places, values, x, hot, held=None):
     rows, width = x.shape
-    chunks = 8
+    chunks, count = 8, len(places)
     first = held is None
     more = [] if first else list(held)
     return pl.pallas_call(
-        functools.partial(apply_body, first, chunks, place),
+        functools.partial(apply_body, first, chunks, places),
         out_shape=[jax.ShapeDtypeStruct((LEAVES, width), F32), jax.ShapeDtypeStruct((rows, width), F32)],
-        in_specs=[IN_VMEM] * 3 + [IN_ANY] * len(more),
+        in_specs=[IN_VMEM] * (2 + count) + [IN_ANY] * len(more),
         out_specs=[IN_ANY] * 2,
-        scratch_shapes=[pltpu.VMEM((rows, LANE), F32), pltpu.SemaphoreType.DMA((chunks + 1,))],
-        input_output_aliases={} if first else {3: 0, 4: 1},
-        compiler_params=params(6),
-        cost_estimate=pl.CostEstimate(flops=4 * rows * LEAVES * LANE, bytes_accessed=8 * rows * LANE, transcendentals=0),
-        name="apply_block",
-    )(value, x, hot, *more)
+        scratch_shapes=[
+            pltpu.VMEM((count, rows, LANE), F32),
+            pltpu.SemaphoreType.DMA((chunks, count)),
+            pltpu.SemaphoreType.DMA((count,)),
+        ],
+        input_output_aliases={} if first else {2 + count: 0, 3 + count: 1},
+        compiler_params=params(4 + 3 * count),
+        cost_estimate=pl.CostEstimate(
+            flops=4 * count * rows * LEAVES * LANE, bytes_accessed=4 * count * rows * LANE, transcendentals=0
+        ),
+        name="apply_blocks",
+    )(x, hot, *values, *more)
 
 
 def newton(sums):
@@ -220,7 +234,7 @@
     hot_cols, hot_rows, classes = index_forms(width, leaf_index, labels)
 
     planes = n_rows == 16 and blocks == 4
-    order = [1, 3, 2, 0] if planes else list(range(blocks))
+    order = [3, 1, 2, 0] if planes else list(range(blocks))
     where = [(planes, d) for d in order]
     scale = None
     parts = []
@@ -228,22 +242,27 @@
         if scale is None:
             part, scale = leaf_sums(block, e, hot_cols, classes, stats=stats)
         else:
-            part = leaf_sums(block, e, hot_cols, classes, scale=scale)
+            part = leaf_sums(block, e, hot_cols, classes, scale=scale, after=parts[-1])
         parts.append(part)
 
     if planes:
         got = [swap(part, d) for part, d in zip(parts[:3], order[:3])]
-        sums = parts[3] + got[0] + got[1] + got[2]
+        sums = parts[3]
+        for part in got:
+            sums = lax.optimization_barrier(sums + part)
         sums = sums + swap(sums, 4)
         sums = sums + swap(sums, 8)
         value = newton(sums)
-        values = [(where[3], value)] + [(w, swap(value, d)) for w, d in zip(where[:3], order[:3])]
-    else:
-        values = list(zip(where, [newton(s) for s in lax.psum(parts, "rows")]))
-
-    held = None
-    for block, value in values:
-        held = apply_block(block, value, x, hot_rows, held)
+        values = [swap(value, d) for d in order[:3]] + [value]
+    else:
+        values = [newton(s) for s in lax.psum(parts, "rows")]
+
+    if planes:
+        held = apply_blocks(where[3:], values[3:], x, hot_rows)
+        held = apply_blocks(where[:1], values[:1], x, hot_rows, held)
+        held = apply_blocks(where[1:3], values[1:3], x, hot_rows, held)
+    else:
+        held = apply_blocks(where, values, x, hot_rows)
     return held[0], held[1]
 
 

time: 45.2 us -> 41.6 us (0.920)
  waiting for transfers between devices: 14.8 us -> 12.1 us
  Pallas kernels: 16.7 us -> 15.8 us
    ppermute x8, waiting for transfers between devices: 14.8 us -> 12.1 us  [swap(): return lax.ppermute(value, 'rows', [(i, i ^ bit) for i in range(n_rows)])]
    pallas_call x4 -> x3, Pallas kernels: 6.93 us -> 6.05 us  [apply_blocks(): pl.pallas_call(functools.partial(apply_body, first, chunks, places), out_...]
  transfers between devices with their start and end apart: 9 -> 9, of which waited for: 5 -> 4; matrix products, arithmetic and copies ran while one was open for 0% -> 0% of each run, Pallas kernels for 17% -> 20%
where the time goes in v3:
time: 41.6 us; the launch traced here: 41.5 us
  Pallas kernels  15.8 us (38%)
  starting transfers between devices  12.6 us (30%)
  waiting for transfers between devices  12.1 us (29%)
  between operations  0.8 us (2%)
    ppermute x8, waiting for transfers between devices, swap(): return lax.ppermute(value, 'rows', [(i, i ^ bit) for i in range(n_rows)])  12.1 us
    ppermute x8, starting transfers between devices, swap(): return lax.ppermute(value, 'rows', [(i, i ^ bit) for i in range(n_rows)])  12.1 us
    pallas_call x3, Pallas kernels, apply_blocks(): pl.pallas_call(functools.partial(apply_body, first, chunks, places), out_...  6.05 us
    pallas_call x4, Pallas kernels, leaf_sums(): pl.pallas_call(functools.partial(sums_body, first, len(more) // 2, place)...  4.72 us
    pallas_call x1, Pallas kernels, local_stats(): pl.pallas_call(functools.partial(stats_body, chunks), out_shape=[full, fu...  3.88 us
    pallas_call x1, Pallas kernels, index_forms(): pl.pallas_call(functools.partial(index_body, width), out_shape=[pltpu.VME...  1.18 us
  transfers between devices with their start and end apart: 9, of which 4 were waited for; matrix products, arithmetic and copies ran while one was open for 0% of the time, Pallas kernels for 20%

profile of v3, /device:TPU:0, one launch (start us, length us, event | category | flops | bytes accessed | tf_op | source)
XLA Modules:
  0.0 41.5 jit_solution(3043014111440746506)
XLA Ops:
  0.6 0.0 copy-start
  0.6 0.0 copy-start.1
  0.6 3.9 %local_stats.1 = (f32[4096,512]{1,0:T(8,128)S(1)}, f32[4096,512]{1,0:T(8,128)S(1)}, f32[32,128]{1,0:T(8,128)S(1)}, f32[32,128]{1,0:T(8,128)S(1)}) custom-call(f32[4096,512]{1,0:T(8,128)} %x_hbm.1), custom_call_target="tpu_custom_call" | custom-call | flops 12582912 | bytes 8388608 | tf_op jit(solution)/shard_map/local_stats/pallas_call | solution.py:57
  4.5 0.5 %collective-permute-start = (f32[2,32,128]{2,1,0:T(8,128)S(1)}, f32[2,32,128]{2,1,0:T(8,128)S(1)}, u32[]{:S(2)}, u32[]{:S(2)}) collective-permute-start(f32[2,32,128]{2,1,0:T(8,128)S(1)} %pad_maximum_fusion), channel_id=1, source_target_pairs={{0,1},{1,0},{2,3},{3,2},{4,5},{5,4},{6,7},{7,6},{8,9},{9,8},{10,11... | collective-permute-start | bytes 98312 | tf_op jit(solution)/shard_map/ppermute | solution.py:233
  5.1 0.0 copy-done
  5.1 0.0 copy-done.1
  5.1 1.2 %index_forms.1 = (bf16[128,4096]{1,0:T(8,128)(2,1)S(1)}, bf16[4096,128]{1,0:T(8,128)(2,1)S(1)}, s32[4096,128]{1,0:T(8,128)S(1)}) custom-call(s32[32,128]{1,0:T(8,128)S(1)} %bitcast.10, s32[32,128]{1,0:T(8,128)S(1)} %bitcast.11), custom_call_target="tpu_custom_call" | custom-call | tf_op jit(solution)/shard_map/index_forms/pallas_call | solution.py:85
  6.3 0.0 collective-permute-done
  6.3 1.2 %leaf_sums.4 = (f32[256,128]{1,0:T(8,128)S(1)}, f32[4096,128]{1,0:T(8,128)S(1)}) custom-call(f32[4096,512]{1,0:T(8,128)S(1)} %get-tuple-element.17.e_ref, bf16[128,4096]{1,0:T(8,128)(2,1)S(1)} %get-tuple-element.18.hot_ref, s32[4096,128]{1,0:T(8,128)S(1)} %get-tuple-element.19.class_ref, f32[32,128]{1,0:T(8,128)S(1)} %get-tuple-element.20.refs_0_, ...), custom_call_target="tpu_custom_call" | custom-call | flops 1 | bytes 1 | tf_op jit(solution)/shard_map/leaf_sums/pallas_call | solution.py:148
  7.5 3.5 %collective-permute-start.1 = (f32[256,128]{1,0:T(8,128)S(1)}, f32[256,128]{1,0:T(8,128)S(1)}, u32[]{:S(2)}, u32[]{:S(2)}) collective-permute-start(f32[256,128]{1,0:T(8,128)S(1)} %get-tuple-element.23.refs_1_), channel_id=1, source_target_pairs={{0,6},{2,4},{4,2},{6,0},{8,14},{10,12},{12,10},{14,8},{16,22},{18,... | collective-permute-start | bytes 393224 | tf_op jit(solution)/shard_map/ppermute | solution.py:227
  11.0 1.1 %leaf_sums.5.refs_1_ = f32[256,128]{1,0:T(8,128)S(1)} custom-call(f32[4096,512]{1,0:T(8,128)S(1)} %get-tuple-element.17.e_ref, bf16[128,4096]{1,0:T(8,128)(2,1)S(1)} %get-tuple-element.18.hot_ref, s32[4096,128]{1,0:T(8,128)S(1)} %get-tuple-element.19.class_ref, f32[4096,128]{1,0:T(8,128)S(1)} %get-tuple-element.22.refs_0_, ...), custom_call_target="tpu_custom_call" | custom-call | flops 1 | bytes 1 | tf_op jit(solution)/shard_map/leaf_sums/pallas_call | solution.py:148
  12.2 0.6 %collective-permute-start.2 = (f32[256,128]{1,0:T(8,128)S(1)}, f32[256,128]{1,0:T(8,128)S(1)}, u32[]{:S(2)}, u32[]{:S(2)}) collective-permute-start(f32[256,128]{1,0:T(8,128)S(1)} %leaf_sums.5.refs_1_), channel_id=1, source_target_pairs={{0,2},{2,0},{4,6},{6,4},{8,10},{10,8},{12,14},{14,12},{16,18},{18,... | collective-permute-start | bytes 393224 | tf_op jit(solution)/shard_map/ppermute | solution.py:227
  12.7 1.2 %leaf_sums.6.refs_1_ = f32[256,128]{1,0:T(8,128)S(1)} custom-call(f32[4096,512]{1,0:T(8,128)S(1)} %get-tuple-element.17.e_ref, bf16[128,4096]{1,0:T(8,128)(2,1)S(1)} %get-tuple-element.18.hot_ref, s32[4096,128]{1,0:T(8,128)S(1)} %get-tuple-element.19.class_ref, f32[4096,128]{1,0:T(8,128)S(1)} %get-tuple-element.22.refs_0_, f32[256,128]{1,0:T(8,128)S(1)} %leaf_sums.5.refs_1_), custom_call_target="tpu_custom_call" | custom-call | flops 1 | bytes 1 | tf_op jit(solution)/shard_map/leaf_sums/pallas_call | solution.py:148
  14.0 0.1 collective-permute-start.3
  14.1 1.1 %leaf_sums.7 = f32[256,128]{1,0:T(8,128)S(1)} custom-call(f32[4096,512]{1,0:T(8,128)S(1)} %get-tuple-element.17.e_ref, bf16[128,4096]{1,0:T(8,128)(2,1)S(1)} %get-tuple-element.18.hot_ref, s32[4096,128]{1,0:T(8,128)S(1)} %get-tuple-element.19.class_ref, f32[4096,128]{1,0:T(8,128)S(1)} %get-tuple-element.22.refs_0_, f32[256,128]{1,0:T(8,128)S(1)} %leaf_sums.6.refs_1_), custom_call_target="tpu_custom_call" | custom-call | flops 1 | bytes 1 | tf_op jit(solution)/shard_map/leaf_sums/pallas_call | solution.py:148
  15.3 0.0 collective-permute-done.1
  15.3 2.9 %collective-permute-done.2 = f32[256,128]{1,0:T(8,128)S(1)} collective-permute-done((f32[256,128]{1,0:T(8,128)S(1)}, f32[256,128]{1,0:T(8,128)S(1)}, u32[]{:S(2)}, u32[]{:S(2)}) %collective-permute-start.2) | collective-permute-done | bytes 131104 | tf_op jit(solution)/shard_map/ppermute | solution.py:227
  18.2 1.2 %collective-permute-done.3 = f32[256,128]{1,0:T(8,128)S(1)} collective-permute-done((f32[256,128]{1,0:T(8,128)S(1)}, f32[256,128]{1,0:T(8,128)S(1)}, u32[]{:S(2)}, u32[]{:S(2)}) %collective-permute-start.3) | collective-permute-done | bytes 131104 | tf_op jit(solution)/shard_map/ppermute | solution.py:227
  19.4 1.6 %collective-permute-start.4 = (f32[256,128]{1,0:T(8,128)S(1)}, f32[256,128]{1,0:T(8,128)S(1)}, u32[]{:S(2)}, u32[]{:S(2)}) collective-permute-start(f32[256,128]{1,0:T(8,128)S(1)} %add.23), channel_id=1, source_target_pairs={{0,8},{2,10},{4,12},{6,14},{8,0},{10,2},{12,4},{14,6},{16,24},{18,... | collective-permute-start | bytes 393224 | tf_op jit(solution)/shard_map/ppermute | solution.py:227
  21.0 3.4 %collective-permute-done.4 = f32[256,128]{1,0:T(8,128)S(1)} collective-permute-done((f32[256,128]{1,0:T(8,128)S(1)}, f32[256,128]{1,0:T(8,128)S(1)}, u32[]{:S(2)}, u32[]{:S(2)}) %collective-permute-start.4) | collective-permute-done | bytes 131104 | tf_op jit(solution)/shard_map/ppermute | solution.py:227
  24.4 2.7 %collective-permute-start.5 = (f32[256,128]{1,0:T(8,128)S(1)}, f32[256,128]{1,0:T(8,128)S(1)}, u32[]{:S(2)}, u32[]{:S(2)}) collective-permute-start(f32[256,128]{1,0:T(8,128)S(1)} %add.24), channel_id=1, source_target_pairs={{0,16},{2,18},{4,20},{6,22},{8,24},{10,26},{12,28},{14,30},{16,0},... | collective-permute-start | bytes 393224 | tf_op jit(solution)/shard_map/ppermute | solution.py:227
  27.1 4.7 %collective-permute-done.5 = f32[256,128]{1,0:T(8,128)S(1)} collective-permute-done((f32[256,128]{1,0:T(8,128)S(1)}, f32[256,128]{1,0:T(8,128)S(1)}, u32[]{:S(2)}, u32[]{:S(2)}) %collective-permute-start.5) | collective-permute-done | bytes 131104 | tf_op jit(solution)/shard_map/ppermute | solution.py:227
  31.8 1.6 %collective-permute-start.8 = (f32[128,128]{1,0:T(8,128)S(1)}, f32[128,128]{1,0:T(8,128)S(1)}, u32[]{:S(2)}, u32[]{:S(2)}) collective-permute-start(f32[128,128]{1,0:T(8,128)S(1)} %fusion.refs_0_), channel_id=1, source_target_pairs={{0,6},{2,4},{4,2},{6,0},{8,14},{10,12},{12,10},{14,8},{16,22},{18,... | collective-permute-start | bytes 196616 | tf_op jit(solution)/shard_map/ppermute | solution.py:227
  33.4 0.6 %collective-permute-start.6 = (f32[128,128]{1,0:T(8,128)S(1)}, f32[128,128]{1,0:T(8,128)S(1)}, u32[]{:S(2)}, u32[]{:S(2)}) collective-permute-start(f32[128,128]{1,0:T(8,128)S(1)} %fusion.refs_0_), channel_id=1, source_target_pairs={{0,2},{2,0},{4,6},{6,4},{8,10},{10,8},{12,14},{14,12},{16,18},{18,... | collective-permute-start | bytes 196616 | tf_op jit(solution)/shard_map/ppermute | solution.py:227
  34.0 1.4 %collective-permute-start.7 = (f32[128,128]{1,0:T(8,128)S(1)}, f32[128,128]{1,0:T(8,128)S(1)}, u32[]{:S(2)}, u32[]{:S(2)}) collective-permute-start(f32[128,128]{1,0:T(8,128)S(1)} %fusion.refs_0_), channel_id=1, source_target_pairs={{0,4},{2,6},{4,0},{6,2},{8,12},{10,14},{12,8},{14,10},{16,20},{18,... | collective-permute-start | bytes 196616 | tf_op jit(solution)/shard_map/ppermute | solution.py:227
  35.4 1.7 %apply_blocks.3 = (f32[128,512]{1,0:T(8,128)}, f32[4096,512]{1,0:T(8,128)}) custom-call(f32[4096,512]{1,0:T(8,128)S(1)} %get-tuple-element.15.x_ref, bf16[4096,128]{1,0:T(8,128)(2,1)S(1)} %get-tuple-element.16.hot_ref, f32[128,128]{1,0:T(8,128)S(1)} %fusion.refs_0_), custom_call_target="tpu_custom_call" | custom-call | flops 268435456 | bytes 2097152 | tf_op jit(solution)/shard_map/apply_blocks/pallas_call | solution.py:199
  37.1 0.0 collective-permute-done.8.refs_0_
  37.1 1.7 %apply_blocks.4 = (f32[128,512]{1,0:T(8,128)}, f32[4096,512]{1,0:T(8,128)}) custom-call(f32[4096,512]{1,0:T(8,128)S(1)} %get-tuple-element.15.x_ref, bf16[4096,128]{1,0:T(8,128)(2,1)S(1)} %get-tuple-element.16.hot_ref, f32[128,128]{1,0:T(8,128)S(1)} %collective-permute-done.8.refs_0_, ...), custom_call_target="tpu_custom_call", output_to_operand_aliasing={{0}: (3, {}), {1}: (4, {})} | custom-call | flops 268435456 | bytes 2097152 | tf_op jit(solution)/shard_map/apply_blocks/pallas_call | solution.py:199
  38.9 0.0 collective-permute-done.6.refs_0_
  38.9 0.0 collective-permute-done.7.refs_1_
  38.9 2.6 %apply_blocks.5 = (f32[128,512]{1,0:T(8,128)}, f32[4096,512]{1,0:T(8,128)}) custom-call(f32[4096,512]{1,0:T(8,128)S(1)} %get-tuple-element.15.x_ref, bf16[4096,128]{1,0:T(8,128)(2,1)S(1)} %get-tuple-element.16.hot_ref, f32[128,128]{1,0:T(8,128)S(1)} %collective-permute-done.6.refs_0_, ...), custom_call_target="tpu_custom_call", output_to_operand_aliasing={{0}: (4, {}), {1}: (5, {})} | custom-call | flops 536870912 | bytes 4194304 | tf_op jit(solution)/shard_map/apply_blocks/pallas_call | solution.py:199
  (8 shorter events, 0.1 us)
Async XLA Ops:
  0.6 4.4 %copy-start = (s32[4096]{0:T(1024)S(1)}, s32[4096]{0:T(1024)}, u32[]{:S(2)}) copy-start(s32[4096]{0:T(1024)} %param.4) | copy-start | bytes 49156
  0.6 4.4 %copy-start.1 = (s32[4096]{0:T(1024)S(1)}, s32[4096]{0:T(1024)}, u32[]{:S(2)}) copy-start(s32[4096]{0:T(1024)} %param.5) | copy-start | bytes 49156
  4.5 1.7 %collective-permute-start = (f32[2,32,128]{2,1,0:T(8,128)S(1)}, f32[2,32,128]{2,1,0:T(8,128)S(1)}, u32[]{:S(2)}, u32[]{:S(2)}) collective-permute-start(f32[2,32,128]{2,1,0:T(8,128)S(1)} %pad_maximum_fusion), channel_id=1, source_target_pairs={{0,1},{1,0},{2,3},{3,2},{4,5},{5,4},{6,7},{7,6},{8,9},{9,8},{10,11... | collective-permute-start | bytes 98312 | tf_op jit(solution)/shard_map/ppermute | solution.py:233
  7.5 7.8 %collective-permute-start.1 = (f32[256,128]{1,0:T(8,128)S(1)}, f32[256,128]{1,0:T(8,128)S(1)}, u32[]{:S(2)}, u32[]{:S(2)}) collective-permute-start(f32[256,128]{1,0:T(8,128)S(1)} %get-tuple-element.23.refs_1_), channel_id=1, source_target_pairs={{0,6},{2,4},{4,2},{6,0},{8,14},{10,12},{12,10},{14,8},{16,22},{18,... | collective-permute-start | bytes 393224 | tf_op jit(solution)/shard_map/ppermute | solution.py:227
  12.2 6.0 %collective-permute-start.2 = (f32[256,128]{1,0:T(8,128)S(1)}, f32[256,128]{1,0:T(8,128)S(1)}, u32[]{:S(2)}, u32[]{:S(2)}) collective-permute-start(f32[256,128]{1,0:T(8,128)S(1)} %leaf_sums.5.refs_1_), channel_id=1, source_target_pairs={{0,2},{2,0},{4,6},{6,4},{8,10},{10,8},{12,14},{14,12},{16,18},{18,... | collective-permute-start | bytes 393224 | tf_op jit(solution)/shard_map/ppermute | solution.py:227
  14.0 5.4 %collective-permute-start.3 = (f32[256,128]{1,0:T(8,128)S(1)}, f32[256,128]{1,0:T(8,128)S(1)}, u32[]{:S(2)}, u32[]{:S(2)}) collective-permute-start(f32[256,128]{1,0:T(8,128)S(1)} %leaf_sums.6.refs_1_), channel_id=1, source_target_pairs={{0,4},{2,6},{4,0},{6,2},{8,12},{10,14},{12,8},{14,10},{16,20},{18,... | collective-permute-start | bytes 393224 | tf_op jit(solution)/shard_map/ppermute | solution.py:227
  19.4 5.0 %collective-permute-start.4 = (f32[256,128]{1,0:T(8,128)S(1)}, f32[256,128]{1,0:T(8,128)S(1)}, u32[]{:S(2)}, u32[]{:S(2)}) collective-permute-start(f32[256,128]{1,0:T(8,128)S(1)} %add.23), channel_id=1, source_target_pairs={{0,8},{2,10},{4,12},{6,14},{8,0},{10,2},{12,4},{14,6},{16,24},{18,... | collective-permute-start | bytes 393224 | tf_op jit(solution)/shard_map/ppermute | solution.py:227
  24.4 7.3 %collective-permute-start.5 = (f32[256,128]{1,0:T(8,128)S(1)}, f32[256,128]{1,0:T(8,128)S(1)}, u32[]{:S(2)}, u32[]{:S(2)}) collective-permute-start(f32[256,128]{1,0:T(8,128)S(1)} %add.24), channel_id=1, source_target_pairs={{0,16},{2,18},{4,20},{6,22},{8,24},{10,26},{12,28},{14,30},{16,0},... | collective-permute-start | bytes 393224 | tf_op jit(solution)/shard_map/ppermute | solution.py:227
  31.8 5.3 %collective-permute-start.8 = (f32[128,128]{1,0:T(8,128)S(1)}, f32[128,128]{1,0:T(8,128)S(1)}, u32[]{:S(2)}, u32[]{:S(2)}) collective-permute-start(f32[128,128]{1,0:T(8,128)S(1)} %fusion.refs_0_), channel_id=1, source_target_pairs={{0,6},{2,4},{4,2},{6,0},{8,14},{10,12},{12,10},{14,8},{16,22},{18,... | collective-permute-start | bytes 196616 | tf_op jit(solution)/shard_map/ppermute | solution.py:227
  33.4 5.4 %collective-permute-start.6 = (f32[128,128]{1,0:T(8,128)S(1)}, f32[128,128]{1,0:T(8,128)S(1)}, u32[]{:S(2)}, u32[]{:S(2)}) collective-permute-start(f32[128,128]{1,0:T(8,128)S(1)} %fusion.refs_0_), channel_id=1, source_target_pairs={{0,2},{2,0},{4,6},{6,4},{8,10},{10,8},{12,14},{14,12},{16,18},{18,... | collective-permute-start | bytes 196616 | tf_op jit(solution)/shard_map/ppermute | solution.py:227
  34.0 4.9 %collective-permute-start.7 = (f32[128,128]{1,0:T(8,128)S(1)}, f32[128,128]{1,0:T(8,128)S(1)}, u32[]{:S(2)}, u32[]{:S(2)}) collective-permute-start(f32[128,128]{1,0:T(8,128)S(1)} %fusion.refs_0_), channel_id=1, source_target_pairs={{0,4},{2,6},{4,0},{6,2},{8,12},{10,14},{12,8},{14,10},{16,20},{18,... | collective-permute-start | bytes 196616 | tf_op jit(solution)/shard_map/ppermute | solution.py:227

commit v4 on v3

--- a/solution.py
+++ b/solution.py
@@ -98,8 +98,8 @@
 
 def block_start(planes, block):
     if planes:
-        block = (lax.axis_index("rows") & 3) ^ block
-        return pl.multiple_of(block * LANE, LANE)
+        far = jnp.where(lax.axis_index("cls") == 0, *block)
+        return pl.multiple_of(((lax.axis_index("rows") & 3) ^ far) * LANE, LANE)
     return block * LANE
 
 
@@ -223,8 +223,9 @@
     width = logits.shape[1]
     blocks = width // LANE
 
-    def swap(value, bit):
-        return lax.ppermute(value, "rows", [(i, i ^ bit) for i in range(n_rows)])
+    def swap(value, far):
+        pairs = [(row * n_cls + core, (row ^ far[core]) * n_cls + core) for row in range(n_rows) for core in range(n_cls)]
+        return lax.ppermute(value, ("rows", "cls"), pairs)
 
     x, e, peak, total = local_stats(logits)
     mine = jnp.stack([peak, total])
@@ -233,8 +234,8 @@
         stats.append(lax.ppermute(mine, "cls", [(i, (i + shift) % n_cls) for i in range(n_cls)]))
     hot_cols, hot_rows, classes = index_forms(width, leaf_index, labels)
 
-    planes = n_rows == 16 and blocks == 4
-    order = [3, 1, 2, 0] if planes else list(range(blocks))
+    planes = n_rows == 16 and n_cls == 2 and blocks == 4
+    order = [(3, 3), (1, 1), (2, 2), (0, 0)] if planes else list(range(blocks))
     where = [(planes, d) for d in order]
     scale = None
     parts = []
@@ -246,14 +247,14 @@
         parts.append(part)
 
     if planes:
-        got = [swap(part, d) for part, d in zip(parts[:3], order[:3])]
+        got = [swap(part, far) for part, far in zip(parts[:3], order[:3])]
         sums = parts[3]
         for part in got:
             sums = lax.optimization_barrier(sums + part)
-        sums = sums + swap(sums, 4)
-        sums = sums + swap(sums, 8)
+        for far in ((4, 8), (8, 4)):
+            sums = sums + swap(sums, far)
         value = newton(sums)
-        values = [swap(value, d) for d in order[:3]] + [value]
+        values = [swap(value, far) for far in order[:3]] + [value]
     else:
         values = [newton(s) for s in lax.psum(parts, "rows")]
 

time: 41.6 us -> 40.4 us (0.971)
  waiting for transfers between devices: 12.1 us -> 10.6 us
    ppermute x8, waiting for transfers between devices: 12.1 us -> 10.6 us  [swap(): return lax.ppermute(value, ('rows', 'cls'), pairs)]
where the time goes in v4:
time: 40.4 us; the launch traced here: 40.2 us
  Pallas kernels  15.8 us (39%)
  starting transfers between devices  12.8 us (32%)
  waiting for transfers between devices  10.6 us (26%)
  between operations  0.8 us (2%)
    ppermute x8, starting transfers between devices, swap(): return lax.ppermute(value, ('rows', 'cls'), pairs)  12.3 us
    ppermute x8, waiting for transfers between devices, swap(): return lax.ppermute(value, ('rows', 'cls'), pairs)  10.6 us
    pallas_call x3, Pallas kernels, apply_blocks(): pl.pallas_call(functools.partial(apply_body, first, chunks, places), out_...  6.04 us
    pallas_call x4, Pallas kernels, leaf_sums(): pl.pallas_call(functools.partial(sums_body, first, len(more) // 2, place)...  4.72 us
    pallas_call x1, Pallas kernels, local_stats(): pl.pallas_call(functools.partial(stats_body, chunks), out_shape=[full, fu...  3.88 us
    pallas_call x1, Pallas kernels, index_forms(): pl.pallas_call(functools.partial(index_body, width), out_shape=[pltpu.VME...  1.18 us
  transfers between devices with their start and end apart: 9, of which 4 were waited for; matrix products, arithmetic and copies ran while one was open for 0% of the time, Pallas kernels for 20%

profile of v4, /device:TPU:0, one launch (start us, length us, event | category | flops | bytes accessed | tf_op | source)
XLA Modules:
  0.0 40.2 jit_solution(15392903062838932177)
XLA Ops:
  0.6 0.0 copy-start
  0.6 0.0 copy-start.1
  0.6 3.9 %local_stats.1 = (f32[4096,512]{1,0:T(8,128)S(1)}, f32[4096,512]{1,0:T(8,128)S(1)}, f32[32,128]{1,0:T(8,128)S(1)}, f32[32,128]{1,0:T(8,128)S(1)}) custom-call(f32[4096,512]{1,0:T(8,128)} %x_hbm.1), custom_call_target="tpu_custom_call" | custom-call | flops 12582912 | bytes 8388608 | tf_op jit(solution)/shard_map/local_stats/pallas_call | solution.py:57
  4.5 0.5 %collective-permute-start = (f32[2,32,128]{2,1,0:T(8,128)S(1)}, f32[2,32,128]{2,1,0:T(8,128)S(1)}, u32[]{:S(2)}, u32[]{:S(2)}) collective-permute-start(f32[2,32,128]{2,1,0:T(8,128)S(1)} %pad_maximum_fusion), channel_id=1, source_target_pairs={{0,1},{1,0},{2,3},{3,2},{4,5},{5,4},{6,7},{7,6},{8,9},{9,8},{10,11... | collective-permute-start | bytes 98312 | tf_op jit(solution)/shard_map/ppermute | solution.py:234
  5.1 0.0 copy-done
  5.1 0.0 copy-done.1
  5.1 1.2 %index_forms.1 = (bf16[128,4096]{1,0:T(8,128)(2,1)S(1)}, bf16[4096,128]{1,0:T(8,128)(2,1)S(1)}, s32[4096,128]{1,0:T(8,128)S(1)}) custom-call(s32[32,128]{1,0:T(8,128)S(1)} %bitcast.10, s32[32,128]{1,0:T(8,128)S(1)} %bitcast.11), custom_call_target="tpu_custom_call" | custom-call | tf_op jit(solution)/shard_map/index_forms/pallas_call | solution.py:85
  6.3 0.0 collective-permute-done
  6.3 1.2 %leaf_sums.4 = (f32[256,128]{1,0:T(8,128)S(1)}, f32[4096,128]{1,0:T(8,128)S(1)}) custom-call(f32[4096,512]{1,0:T(8,128)S(1)} %get-tuple-element.17.e_ref, bf16[128,4096]{1,0:T(8,128)(2,1)S(1)} %get-tuple-element.18.hot_ref, s32[4096,128]{1,0:T(8,128)S(1)} %get-tuple-element.19.class_ref, f32[32,128]{1,0:T(8,128)S(1)} %get-tuple-element.20.refs_0_, ...), custom_call_target="tpu_custom_call" | custom-call | flops 1 | bytes 1 | tf_op jit(solution)/shard_map/leaf_sums/pallas_call | solution.py:148
  7.5 3.5 %collective-permute-start.1 = (f32[256,128]{1,0:T(8,128)S(1)}, f32[256,128]{1,0:T(8,128)S(1)}, u32[]{:S(2)}, u32[]{:S(2)}) collective-permute-start(f32[256,128]{1,0:T(8,128)S(1)} %get-tuple-element.23.refs_1_), channel_id=1, source_target_pairs={{0,6},{1,7},{2,4},{3,5},{4,2},{5,3},{6,0},{7,1},{8,14},{9,15},{10,... | collective-permute-start | bytes 393224 | tf_op jit(solution)/shard_map/ppermute | solution.py:228
  11.0 1.1 %leaf_sums.5.refs_1_ = f32[256,128]{1,0:T(8,128)S(1)} custom-call(f32[4096,512]{1,0:T(8,128)S(1)} %get-tuple-element.17.e_ref, bf16[128,4096]{1,0:T(8,128)(2,1)S(1)} %get-tuple-element.18.hot_ref, s32[4096,128]{1,0:T(8,128)S(1)} %get-tuple-element.19.class_ref, f32[4096,128]{1,0:T(8,128)S(1)} %get-tuple-element.22.refs_0_, ...), custom_call_target="tpu_custom_call" | custom-call | flops 1 | bytes 1 | tf_op jit(solution)/shard_map/leaf_sums/pallas_call | solution.py:148
  12.2 0.6 %collective-permute-start.2 = (f32[256,128]{1,0:T(8,128)S(1)}, f32[256,128]{1,0:T(8,128)S(1)}, u32[]{:S(2)}, u32[]{:S(2)}) collective-permute-start(f32[256,128]{1,0:T(8,128)S(1)} %leaf_sums.5.refs_1_), channel_id=1, source_target_pairs={{0,2},{1,3},{2,0},{3,1},{4,6},{5,7},{6,4},{7,5},{8,10},{9,11},{10,... | collective-permute-start | bytes 393224 | tf_op jit(solution)/shard_map/ppermute | solution.py:228
  12.7 1.2 %leaf_sums.6.refs_1_ = f32[256,128]{1,0:T(8,128)S(1)} custom-call(f32[4096,512]{1,0:T(8,128)S(1)} %get-tuple-element.17.e_ref, bf16[128,4096]{1,0:T(8,128)(2,1)S(1)} %get-tuple-element.18.hot_ref, s32[4096,128]{1,0:T(8,128)S(1)} %get-tuple-element.19.class_ref, f32[4096,128]{1,0:T(8,128)S(1)} %get-tuple-element.22.refs_0_, f32[256,128]{1,0:T(8,128)S(1)} %leaf_sums.5.refs_1_), custom_call_target="tpu_custom_call" | custom-call | flops 1 | bytes 1 | tf_op jit(solution)/shard_map/leaf_sums/pallas_call | solution.py:148
  14.0 0.1 collective-permute-start.3
  14.1 1.1 %leaf_sums.7 = f32[256,128]{1,0:T(8,128)S(1)} custom-call(f32[4096,512]{1,0:T(8,128)S(1)} %get-tuple-element.17.e_ref, bf16[128,4096]{1,0:T(8,128)(2,1)S(1)} %get-tuple-element.18.hot_ref, s32[4096,128]{1,0:T(8,128)S(1)} %get-tuple-element.19.class_ref, f32[4096,128]{1,0:T(8,128)S(1)} %get-tuple-element.22.refs_0_, f32[256,128]{1,0:T(8,128)S(1)} %leaf_sums.6.refs_1_), custom_call_target="tpu_custom_call" | custom-call | flops 1 | bytes 1 | tf_op jit(solution)/shard_map/leaf_sums/pallas_call | solution.py:148
  15.3 0.0 collective-permute-done.1
  15.3 2.9 %collective-permute-done.2 = f32[256,128]{1,0:T(8,128)S(1)} collective-permute-done((f32[256,128]{1,0:T(8,128)S(1)}, f32[256,128]{1,0:T(8,128)S(1)}, u32[]{:S(2)}, u32[]{:S(2)}) %collective-permute-start.2) | collective-permute-done | bytes 131104 | tf_op jit(solution)/shard_map/ppermute | solution.py:228
  18.2 1.2 %collective-permute-done.3 = f32[256,128]{1,0:T(8,128)S(1)} collective-permute-done((f32[256,128]{1,0:T(8,128)S(1)}, f32[256,128]{1,0:T(8,128)S(1)}, u32[]{:S(2)}, u32[]{:S(2)}) %collective-permute-start.3) | collective-permute-done | bytes 131104 | tf_op jit(solution)/shard_map/ppermute | solution.py:228
  19.4 1.6 %collective-permute-start.4 = (f32[256,128]{1,0:T(8,128)S(1)}, f32[256,128]{1,0:T(8,128)S(1)}, u32[]{:S(2)}, u32[]{:S(2)}) collective-permute-start(f32[256,128]{1,0:T(8,128)S(1)} %add.23), channel_id=1, source_target_pairs={{0,8},{1,17},{2,10},{3,19},{4,12},{5,21},{6,14},{7,23},{8,0},{9,25... | collective-permute-start | bytes 393224 | tf_op jit(solution)/shard_map/ppermute | solution.py:228
  21.0 3.5 %collective-permute-done.4 = f32[256,128]{1,0:T(8,128)S(1)} collective-permute-done((f32[256,128]{1,0:T(8,128)S(1)}, f32[256,128]{1,0:T(8,128)S(1)}, u32[]{:S(2)}, u32[]{:S(2)}) %collective-permute-start.4) | collective-permute-done | bytes 131104 | tf_op jit(solution)/shard_map/ppermute | solution.py:228
  24.6 2.9 %collective-permute-start.5 = (f32[256,128]{1,0:T(8,128)S(1)}, f32[256,128]{1,0:T(8,128)S(1)}, u32[]{:S(2)}, u32[]{:S(2)}) collective-permute-start(f32[256,128]{1,0:T(8,128)S(1)} %add.24), channel_id=1, source_target_pairs={{0,16},{1,9},{2,18},{3,11},{4,20},{5,13},{6,22},{7,15},{8,24},{9,1... | collective-permute-start | bytes 393224 | tf_op jit(solution)/shard_map/ppermute | solution.py:228
  27.5 3.0 %collective-permute-done.5 = f32[256,128]{1,0:T(8,128)S(1)} collective-permute-done((f32[256,128]{1,0:T(8,128)S(1)}, f32[256,128]{1,0:T(8,128)S(1)}, u32[]{:S(2)}, u32[]{:S(2)}) %collective-permute-start.5) | collective-permute-done | bytes 131104 | tf_op jit(solution)/shard_map/ppermute | solution.py:228
  30.5 1.7 %collective-permute-start.8 = (f32[128,128]{1,0:T(8,128)S(1)}, f32[128,128]{1,0:T(8,128)S(1)}, u32[]{:S(2)}, u32[]{:S(2)}) collective-permute-start(f32[128,128]{1,0:T(8,128)S(1)} %fusion.refs_0_), channel_id=1, source_target_pairs={{0,6},{1,7},{2,4},{3,5},{4,2},{5,3},{6,0},{7,1},{8,14},{9,15},{10,... | collective-permute-start | bytes 196616 | tf_op jit(solution)/shard_map/ppermute | solution.py:228
  32.2 0.4 collective-permute-start.6
  32.6 1.5 %collective-permute-start.7 = (f32[128,128]{1,0:T(8,128)S(1)}, f32[128,128]{1,0:T(8,128)S(1)}, u32[]{:S(2)}, u32[]{:S(2)}) collective-permute-start(f32[128,128]{1,0:T(8,128)S(1)} %fusion.refs_0_), channel_id=1, source_target_pairs={{0,4},{1,5},{2,6},{3,7},{4,0},{5,1},{6,2},{7,3},{8,12},{9,13},{10,... | collective-permute-start | bytes 196616 | tf_op jit(solution)/shard_map/ppermute | solution.py:228
  34.1 1.7 %apply_blocks.3 = (f32[128,512]{1,0:T(8,128)}, f32[4096,512]{1,0:T(8,128)}) custom-call(f32[4096,512]{1,0:T(8,128)S(1)} %get-tuple-element.15.x_ref, bf16[4096,128]{1,0:T(8,128)(2,1)S(1)} %get-tuple-element.16.hot_ref, f32[128,128]{1,0:T(8,128)S(1)} %fusion.refs_0_), custom_call_target="tpu_custom_call" | custom-call | flops 268435456 | bytes 2097152 | tf_op jit(solution)/shard_map/apply_blocks/pallas_call | solution.py:199
  35.8 0.0 collective-permute-done.8.refs_0_
  35.8 1.7 %apply_blocks.4 = (f32[128,512]{1,0:T(8,128)}, f32[4096,512]{1,0:T(8,128)}) custom-call(f32[4096,512]{1,0:T(8,128)S(1)} %get-tuple-element.15.x_ref, bf16[4096,128]{1,0:T(8,128)(2,1)S(1)} %get-tuple-element.16.hot_ref, f32[128,128]{1,0:T(8,128)S(1)} %collective-permute-done.8.refs_0_, ...), custom_call_target="tpu_custom_call", output_to_operand_aliasing={{0}: (3, {}), {1}: (4, {})} | custom-call | flops 268435456 | bytes 2097152 | tf_op jit(solution)/shard_map/apply_blocks/pallas_call | solution.py:199
  37.6 0.0 collective-permute-done.6.refs_0_
  37.6 0.0 collective-permute-done.7.refs_1_
  37.6 2.6 %apply_blocks.5 = (f32[128,512]{1,0:T(8,128)}, f32[4096,512]{1,0:T(8,128)}) custom-call(f32[4096,512]{1,0:T(8,128)S(1)} %get-tuple-element.15.x_ref, bf16[4096,128]{1,0:T(8,128)(2,1)S(1)} %get-tuple-element.16.hot_ref, f32[128,128]{1,0:T(8,128)S(1)} %collective-permute-done.6.refs_0_, ...), custom_call_target="tpu_custom_call", output_to_operand_aliasing={{0}: (4, {}), {1}: (5, {})} | custom-call | flops 536870912 | bytes 4194304 | tf_op jit(solution)/shard_map/apply_blocks/pallas_call | solution.py:199
  (8 shorter events, 0.1 us)
Async XLA Ops:
  0.6 4.4 %copy-start = (s32[4096]{0:T(1024)S(1)}, s32[4096]{0:T(1024)}, u32[]{:S(2)}) copy-start(s32[4096]{0:T(1024)} %param.4) | copy-start | bytes 49156
  0.6 4.4 %copy-start.1 = (s32[4096]{0:T(1024)S(1)}, s32[4096]{0:T(1024)}, u32[]{:S(2)}) copy-start(s32[4096]{0:T(1024)} %param.5) | copy-start | bytes 49156
  4.5 1.7 %collective-permute-start = (f32[2,32,128]{2,1,0:T(8,128)S(1)}, f32[2,32,128]{2,1,0:T(8,128)S(1)}, u32[]{:S(2)}, u32[]{:S(2)}) collective-permute-start(f32[2,32,128]{2,1,0:T(8,128)S(1)} %pad_maximum_fusion), channel_id=1, source_target_pairs={{0,1},{1,0},{2,3},{3,2},{4,5},{5,4},{6,7},{7,6},{8,9},{9,8},{10,11... | collective-permute-start | bytes 98312 | tf_op jit(solution)/shard_map/ppermute | solution.py:234
  7.5 7.8 %collective-permute-start.1 = (f32[256,128]{1,0:T(8,128)S(1)}, f32[256,128]{1,0:T(8,128)S(1)}, u32[]{:S(2)}, u32[]{:S(2)}) collective-permute-start(f32[256,128]{1,0:T(8,128)S(1)} %get-tuple-element.23.refs_1_), channel_id=1, source_target_pairs={{0,6},{1,7},{2,4},{3,5},{4,2},{5,3},{6,0},{7,1},{8,14},{9,15},{10,... | collective-permute-start | bytes 393224 | tf_op jit(solution)/shard_map/ppermute | solution.py:228
  12.2 6.0 %collective-permute-start.2 = (f32[256,128]{1,0:T(8,128)S(1)}, f32[256,128]{1,0:T(8,128)S(1)}, u32[]{:S(2)}, u32[]{:S(2)}) collective-permute-start(f32[256,128]{1,0:T(8,128)S(1)} %leaf_sums.5.refs_1_), channel_id=1, source_target_pairs={{0,2},{1,3},{2,0},{3,1},{4,6},{5,7},{6,4},{7,5},{8,10},{9,11},{10,... | collective-permute-start | bytes 393224 | tf_op jit(solution)/shard_map/ppermute | solution.py:228
  14.0 5.4 %collective-permute-start.3 = (f32[256,128]{1,0:T(8,128)S(1)}, f32[256,128]{1,0:T(8,128)S(1)}, u32[]{:S(2)}, u32[]{:S(2)}) collective-permute-start(f32[256,128]{1,0:T(8,128)S(1)} %leaf_sums.6.refs_1_), channel_id=1, source_target_pairs={{0,4},{1,5},{2,6},{3,7},{4,0},{5,1},{6,2},{7,3},{8,12},{9,13},{10,... | collective-permute-start | bytes 393224 | tf_op jit(solution)/shard_map/ppermute | solution.py:228
  19.4 5.2 %collective-permute-start.4 = (f32[256,128]{1,0:T(8,128)S(1)}, f32[256,128]{1,0:T(8,128)S(1)}, u32[]{:S(2)}, u32[]{:S(2)}) collective-permute-start(f32[256,128]{1,0:T(8,128)S(1)} %add.23), channel_id=1, source_target_pairs={{0,8},{1,17},{2,10},{3,19},{4,12},{5,21},{6,14},{7,23},{8,0},{9,25... | collective-permute-start | bytes 393224 | tf_op jit(solution)/shard_map/ppermute | solution.py:228
  24.6 5.9 %collective-permute-start.5 = (f32[256,128]{1,0:T(8,128)S(1)}, f32[256,128]{1,0:T(8,128)S(1)}, u32[]{:S(2)}, u32[]{:S(2)}) collective-permute-start(f32[256,128]{1,0:T(8,128)S(1)} %add.24), channel_id=1, source_target_pairs={{0,16},{1,9},{2,18},{3,11},{4,20},{5,13},{6,22},{7,15},{8,24},{9,1... | collective-permute-start | bytes 393224 | tf_op jit(solution)/shard_map/ppermute | solution.py:228
  30.5 5.3 %collective-permute-start.8 = (f32[128,128]{1,0:T(8,128)S(1)}, f32[128,128]{1,0:T(8,128)S(1)}, u32[]{:S(2)}, u32[]{:S(2)}) collective-permute-start(f32[128,128]{1,0:T(8,128)S(1)} %fusion.refs_0_), channel_id=1, source_target_pairs={{0,6},{1,7},{2,4},{3,5},{4,2},{5,3},{6,0},{7,1},{8,14},{9,15},{10,... | collective-permute-start | bytes 196616 | tf_op jit(solution)/shard_map/ppermute | solution.py:228
  32.2 5.4 %collective-permute-start.6 = (f32[128,128]{1,0:T(8,128)S(1)}, f32[128,128]{1,0:T(8,128)S(1)}, u32[]{:S(2)}, u32[]{:S(2)}) collective-permute-start(f32[128,128]{1,0:T(8,128)S(1)} %fusion.refs_0_), channel_id=1, source_target_pairs={{0,2},{1,3},{2,0},{3,1},{4,6},{5,7},{6,4},{7,5},{8,10},{9,11},{10,... | collective-permute-start | bytes 196616 | tf_op jit(solution)/shard_map/ppermute | solution.py:228
  32.6 5.0 %collective-permute-start.7 = (f32[128,128]{1,0:T(8,128)S(1)}, f32[128,128]{1,0:T(8,128)S(1)}, u32[]{:S(2)}, u32[]{:S(2)}) collective-permute-start(f32[128,128]{1,0:T(8,128)S(1)} %fusion.refs_0_), channel_id=1, source_target_pairs={{0,4},{1,5},{2,6},{3,7},{4,0},{5,1},{6,2},{7,3},{8,12},{9,13},{10,... | collective-permute-start | bytes 196616 | tf_op jit(solution)/shard_map/ppermute | solution.py:228

commit v5 on v4

--- a/solution.py
+++ b/solution.py
@@ -158,17 +158,17 @@
     return got if first else got[0]
 
 
-def apply_body(first, chunks, places, x_ref, hot_ref, *refs):
-    count = len(places)
+def apply_body(first, sizes, places, x_ref, hot_ref, *refs):
+    count, chunks = len(places), len(sizes)
+    starts = [sum(sizes[:i]) for i in range(chunks)]
     values, refs = refs[:count], refs[count:]
     if not first:
         refs = refs[2:]
     value_hbm, updated_hbm, tile_ref, sems, value_sems = refs
     columns = [pl.ds(block_start(*place), LANE) for place in places]
-    step = x_ref.shape[0] // chunks
 
     def send(i, b):
-        at = pl.ds(i * step, step)
+        at = pl.ds(starts[i], sizes[i])
         return pltpu.make_async_copy(tile_ref.at[b, at], updated_hbm.at[at, columns[b]], sems.at[i, b])
 
     def send_value(b):
@@ -178,7 +178,7 @@
         send_value(b).start()
     right = [jnp.concatenate(split(value[...]), axis=0) for value in values]
     for i in range(chunks):
-        at = pl.ds(i * step, step)
+        at = pl.ds(starts[i], sizes[i])
         hot = hot_ref[at]
         left = jnp.concatenate([hot, hot], axis=1)
         for b in range(count):
@@ -193,17 +193,19 @@
 
 def apply_blocks(places, values, x, hot, held=None):
     rows, width = x.shape
-    chunks, count = 8, len(places)
+    count = len(places)
+    step = 4 * LANE
+    sizes = [LANE, step - LANE] + [step] * (rows // step - 2) + [step - LANE, LANE]
     first = held is None
     more = [] if first else list(held)
     return pl.pallas_call(
-        functools.partial(apply_body, first, chunks, places),
+        functools.partial(apply_body, first, sizes, places),
         out_shape=[jax.ShapeDtypeStruct((LEAVES, width), F32), jax.ShapeDtypeStruct((rows, width), F32)],
         in_specs=[IN_VMEM] * (2 + count) + [IN_ANY] * len(more),
         out_specs=[IN_ANY] * 2,
         scratch_shapes=[
             pltpu.VMEM((count, rows, LANE), F32),
-            pltpu.SemaphoreType.DMA((chunks, count)),
+            pltpu.SemaphoreType.DMA((len(sizes), count)),
             pltpu.SemaphoreType.DMA((count,)),
         ],
         input_output_aliases={} if first else {2 + count: 0, 3 + count: 1},

time: 40.4 us -> 40.3 us (level)
  no operation moved by 1% of the time
where the time goes in v5:
time: 40.3 us; the launch traced here: 40 us
  Pallas kernels  15.7 us (39%)
  starting transfers between devices  12.8 us (32%)
  waiting for transfers between devices  10.6 us (26%)
  between operations  0.79 us (2%)
    ppermute x8, starting transfers between devices, swap(): return lax.ppermute(value, ('rows', 'cls'), pairs)  12.3 us
    ppermute x8, waiting for transfers between devices, swap(): return lax.ppermute(value, ('rows', 'cls'), pairs)  10.6 us
    pallas_call x3, Pallas kernels, apply_blocks(): pl.pallas_call(functools.partial(apply_body, first, sizes, places), out_s...  5.9 us
    pallas_call x4, Pallas kernels, leaf_sums(): pl.pallas_call(functools.partial(sums_body, first, len(more) // 2, place)...  4.72 us
    pallas_call x1, Pallas kernels, local_stats(): pl.pallas_call(functools.partial(stats_body, chunks), out_shape=[full, fu...  3.88 us
    pallas_call x1, Pallas kernels, index_forms(): pl.pallas_call(functools.partial(index_body, width), out_shape=[pltpu.VME...  1.18 us
  transfers between devices with their start and end apart: 9, of which 4 were waited for; matrix products, arithmetic and copies ran while one was open for 0% of the time, Pallas kernels for 20%

profile of v5, /device:TPU:0, one launch (start us, length us, event | category | flops | bytes accessed | tf_op | source)
XLA Modules:
  0.0 40.0 jit_solution(302650410703096905)
XLA Ops:
  0.6 0.0 copy-start
  0.6 0.0 copy-start.1
  0.6 3.9 %local_stats.1 = (f32[4096,512]{1,0:T(8,128)S(1)}, f32[4096,512]{1,0:T(8,128)S(1)}, f32[32,128]{1,0:T(8,128)S(1)}, f32[32,128]{1,0:T(8,128)S(1)}) custom-call(f32[4096,512]{1,0:T(8,128)} %x_hbm.1), custom_call_target="tpu_custom_call" | custom-call | flops 12582912 | bytes 8388608 | tf_op jit(solution)/shard_map/local_stats/pallas_call | solution.py:57
  4.5 0.5 %collective-permute-start = (f32[2,32,128]{2,1,0:T(8,128)S(1)}, f32[2,32,128]{2,1,0:T(8,128)S(1)}, u32[]{:S(2)}, u32[]{:S(2)}) collective-permute-start(f32[2,32,128]{2,1,0:T(8,128)S(1)} %pad_maximum_fusion), channel_id=1, source_target_pairs={{0,1},{1,0},{2,3},{3,2},{4,5},{5,4},{6,7},{7,6},{8,9},{9,8},{10,11... | collective-permute-start | bytes 98312 | tf_op jit(solution)/shard_map/ppermute | solution.py:236
  5.1 0.0 copy-done
  5.1 0.0 copy-done.1
  5.1 1.2 %index_forms.1 = (bf16[128,4096]{1,0:T(8,128)(2,1)S(1)}, bf16[4096,128]{1,0:T(8,128)(2,1)S(1)}, s32[4096,128]{1,0:T(8,128)S(1)}) custom-call(s32[32,128]{1,0:T(8,128)S(1)} %bitcast.10, s32[32,128]{1,0:T(8,128)S(1)} %bitcast.11), custom_call_target="tpu_custom_call" | custom-call | tf_op jit(solution)/shard_map/index_forms/pallas_call | solution.py:85
  6.3 0.0 collective-permute-done
  6.3 1.2 %leaf_sums.4 = (f32[256,128]{1,0:T(8,128)S(1)}, f32[4096,128]{1,0:T(8,128)S(1)}) custom-call(f32[4096,512]{1,0:T(8,128)S(1)} %get-tuple-element.17.e_ref, bf16[128,4096]{1,0:T(8,128)(2,1)S(1)} %get-tuple-element.18.hot_ref, s32[4096,128]{1,0:T(8,128)S(1)} %get-tuple-element.19.class_ref, f32[32,128]{1,0:T(8,128)S(1)} %get-tuple-element.20.refs_0_, ...), custom_call_target="tpu_custom_call" | custom-call | flops 1 | bytes 1 | tf_op jit(solution)/shard_map/leaf_sums/pallas_call | solution.py:148
  7.5 3.5 %collective-permute-start.1 = (f32[256,128]{1,0:T(8,128)S(1)}, f32[256,128]{1,0:T(8,128)S(1)}, u32[]{:S(2)}, u32[]{:S(2)}) collective-permute-start(f32[256,128]{1,0:T(8,128)S(1)} %get-tuple-element.23.refs_1_), channel_id=1, source_target_pairs={{0,6},{1,7},{2,4},{3,5},{4,2},{5,3},{6,0},{7,1},{8,14},{9,15},{10,... | collective-permute-start | bytes 393224 | tf_op jit(solution)/shard_map/ppermute | solution.py:230
  11.0 1.1 %leaf_sums.5.refs_1_ = f32[256,128]{1,0:T(8,128)S(1)} custom-call(f32[4096,512]{1,0:T(8,128)S(1)} %get-tuple-element.17.e_ref, bf16[128,4096]{1,0:T(8,128)(2,1)S(1)} %get-tuple-element.18.hot_ref, s32[4096,128]{1,0:T(8,128)S(1)} %get-tuple-element.19.class_ref, f32[4096,128]{1,0:T(8,128)S(1)} %get-tuple-element.22.refs_0_, ...), custom_call_target="tpu_custom_call" | custom-call | flops 1 | bytes 1 | tf_op jit(solution)/shard_map/leaf_sums/pallas_call | solution.py:148
  12.2 0.6 %collective-permute-start.2 = (f32[256,128]{1,0:T(8,128)S(1)}, f32[256,128]{1,0:T(8,128)S(1)}, u32[]{:S(2)}, u32[]{:S(2)}) collective-permute-start(f32[256,128]{1,0:T(8,128)S(1)} %leaf_sums.5.refs_1_), channel_id=1, source_target_pairs={{0,2},{1,3},{2,0},{3,1},{4,6},{5,7},{6,4},{7,5},{8,10},{9,11},{10,... | collective-permute-start | bytes 393224 | tf_op jit(solution)/shard_map/ppermute | solution.py:230
  12.7 1.2 %leaf_sums.6.refs_1_ = f32[256,128]{1,0:T(8,128)S(1)} custom-call(f32[4096,512]{1,0:T(8,128)S(1)} %get-tuple-element.17.e_ref, bf16[128,4096]{1,0:T(8,128)(2,1)S(1)} %get-tuple-element.18.hot_ref, s32[4096,128]{1,0:T(8,128)S(1)} %get-tuple-element.19.class_ref, f32[4096,128]{1,0:T(8,128)S(1)} %get-tuple-element.22.refs_0_, f32[256,128]{1,0:T(8,128)S(1)} %leaf_sums.5.refs_1_), custom_call_target="tpu_custom_call" | custom-call | flops 1 | bytes 1 | tf_op jit(solution)/shard_map/leaf_sums/pallas_call | solution.py:148
  14.0 0.1 collective-permute-start.3
  14.1 1.1 %leaf_sums.7 = f32[256,128]{1,0:T(8,128)S(1)} custom-call(f32[4096,512]{1,0:T(8,128)S(1)} %get-tuple-element.17.e_ref, bf16[128,4096]{1,0:T(8,128)(2,1)S(1)} %get-tuple-element.18.hot_ref, s32[4096,128]{1,0:T(8,128)S(1)} %get-tuple-element.19.class_ref, f32[4096,128]{1,0:T(8,128)S(1)} %get-tuple-element.22.refs_0_, f32[256,128]{1,0:T(8,128)S(1)} %leaf_sums.6.refs_1_), custom_call_target="tpu_custom_call" | custom-call | flops 1 | bytes 1 | tf_op jit(solution)/shard_map/leaf_sums/pallas_call | solution.py:148
  15.3 0.0 collective-permute-done.1
  15.3 2.9 %collective-permute-done.2 = f32[256,128]{1,0:T(8,128)S(1)} collective-permute-done((f32[256,128]{1,0:T(8,128)S(1)}, f32[256,128]{1,0:T(8,128)S(1)}, u32[]{:S(2)}, u32[]{:S(2)}) %collective-permute-start.2) | collective-permute-done | bytes 131104 | tf_op jit(solution)/shard_map/ppermute | solution.py:230
  18.2 1.2 %collective-permute-done.3 = f32[256,128]{1,0:T(8,128)S(1)} collective-permute-done((f32[256,128]{1,0:T(8,128)S(1)}, f32[256,128]{1,0:T(8,128)S(1)}, u32[]{:S(2)}, u32[]{:S(2)}) %collective-permute-start.3) | collective-permute-done | bytes 131104 | tf_op jit(solution)/shard_map/ppermute | solution.py:230
  19.4 1.6 %collective-permute-start.4 = (f32[256,128]{1,0:T(8,128)S(1)}, f32[256,128]{1,0:T(8,128)S(1)}, u32[]{:S(2)}, u32[]{:S(2)}) collective-permute-start(f32[256,128]{1,0:T(8,128)S(1)} %add.23), channel_id=1, source_target_pairs={{0,8},{1,17},{2,10},{3,19},{4,12},{5,21},{6,14},{7,23},{8,0},{9,25... | collective-permute-start | bytes 393224 | tf_op jit(solution)/shard_map/ppermute | solution.py:230
  21.0 3.5 %collective-permute-done.4 = f32[256,128]{1,0:T(8,128)S(1)} collective-permute-done((f32[256,128]{1,0:T(8,128)S(1)}, f32[256,128]{1,0:T(8,128)S(1)}, u32[]{:S(2)}, u32[]{:S(2)}) %collective-permute-start.4) | collective-permute-done | bytes 131104 | tf_op jit(solution)/shard_map/ppermute | solution.py:230
  24.6 2.9 %collective-permute-start.5 = (f32[256,128]{1,0:T(8,128)S(1)}, f32[256,128]{1,0:T(8,128)S(1)}, u32[]{:S(2)}, u32[]{:S(2)}) collective-permute-start(f32[256,128]{1,0:T(8,128)S(1)} %add.24), channel_id=1, source_target_pairs={{0,16},{1,9},{2,18},{3,11},{4,20},{5,13},{6,22},{7,15},{8,24},{9,1... | collective-permute-start | bytes 393224 | tf_op jit(solution)/shard_map/ppermute | solution.py:230
  27.5 3.0 %collective-permute-done.5 = f32[256,128]{1,0:T(8,128)S(1)} collective-permute-done((f32[256,128]{1,0:T(8,128)S(1)}, f32[256,128]{1,0:T(8,128)S(1)}, u32[]{:S(2)}, u32[]{:S(2)}) %collective-permute-start.5) | collective-permute-done | bytes 131104 | tf_op jit(solution)/shard_map/ppermute | solution.py:230
  30.5 1.7 %collective-permute-start.8 = (f32[128,128]{1,0:T(8,128)S(1)}, f32[128,128]{1,0:T(8,128)S(1)}, u32[]{:S(2)}, u32[]{:S(2)}) collective-permute-start(f32[128,128]{1,0:T(8,128)S(1)} %fusion.refs_0_), channel_id=1, source_target_pairs={{0,6},{1,7},{2,4},{3,5},{4,2},{5,3},{6,0},{7,1},{8,14},{9,15},{10,... | collective-permute-start | bytes 196616 | tf_op jit(solution)/shard_map/ppermute | solution.py:230
  32.2 0.4 collective-permute-start.6
  32.6 1.5 %collective-permute-start.7 = (f32[128,128]{1,0:T(8,128)S(1)}, f32[128,128]{1,0:T(8,128)S(1)}, u32[]{:S(2)}, u32[]{:S(2)}) collective-permute-start(f32[128,128]{1,0:T(8,128)S(1)} %fusion.refs_0_), channel_id=1, source_target_pairs={{0,4},{1,5},{2,6},{3,7},{4,0},{5,1},{6,2},{7,3},{8,12},{9,13},{10,... | collective-permute-start | bytes 196616 | tf_op jit(solution)/shard_map/ppermute | solution.py:230
  34.1 1.7 %apply_blocks.3 = (f32[128,512]{1,0:T(8,128)}, f32[4096,512]{1,0:T(8,128)}) custom-call(f32[4096,512]{1,0:T(8,128)S(1)} %get-tuple-element.15.x_ref, bf16[4096,128]{1,0:T(8,128)(2,1)S(1)} %get-tuple-element.16.hot_ref, f32[128,128]{1,0:T(8,128)S(1)} %fusion.refs_0_), custom_call_target="tpu_custom_call" | custom-call | flops 268435456 | bytes 2097152 | tf_op jit(solution)/shard_map/apply_blocks/pallas_call | solution.py:201
  35.8 0.0 collective-permute-done.8.refs_0_
  35.8 1.7 %apply_blocks.4 = (f32[128,512]{1,0:T(8,128)}, f32[4096,512]{1,0:T(8,128)}) custom-call(f32[4096,512]{1,0:T(8,128)S(1)} %get-tuple-element.15.x_ref, bf16[4096,128]{1,0:T(8,128)(2,1)S(1)} %get-tuple-element.16.hot_ref, f32[128,128]{1,0:T(8,128)S(1)} %collective-permute-done.8.refs_0_, ...), custom_call_target="tpu_custom_call", output_to_operand_aliasing={{0}: (3, {}), {1}: (4, {})} | custom-call | flops 268435456 | bytes 2097152 | tf_op jit(solution)/shard_map/apply_blocks/pallas_call | solution.py:201
  37.4 0.0 collective-permute-done.6.refs_0_
  37.5 0.0 collective-permute-done.7.refs_1_
  37.5 2.6 %apply_blocks.5 = (f32[128,512]{1,0:T(8,128)}, f32[4096,512]{1,0:T(8,128)}) custom-call(f32[4096,512]{1,0:T(8,128)S(1)} %get-tuple-element.15.x_ref, bf16[4096,128]{1,0:T(8,128)(2,1)S(1)} %get-tuple-element.16.hot_ref, f32[128,128]{1,0:T(8,128)S(1)} %collective-permute-done.6.refs_0_, ...), custom_call_target="tpu_custom_call", output_to_operand_aliasing={{0}: (4, {}), {1}: (5, {})} | custom-call | flops 536870912 | bytes 4194304 | tf_op jit(solution)/shard_map/apply_blocks/pallas_call | solution.py:201
  (8 shorter events, 0.1 us)
Async XLA Ops:
  0.6 4.4 %copy-start = (s32[4096]{0:T(1024)S(1)}, s32[4096]{0:T(1024)}, u32[]{:S(2)}) copy-start(s32[4096]{0:T(1024)} %param.4) | copy-start | bytes 49156
  0.6 4.4 %copy-start.1 = (s32[4096]{0:T(1024)S(1)}, s32[4096]{0:T(1024)}, u32[]{:S(2)}) copy-start(s32[4096]{0:T(1024)} %param.5) | copy-start | bytes 49156
  4.5 1.7 %collective-permute-start = (f32[2,32,128]{2,1,0:T(8,128)S(1)}, f32[2,32,128]{2,1,0:T(8,128)S(1)}, u32[]{:S(2)}, u32[]{:S(2)}) collective-permute-start(f32[2,32,128]{2,1,0:T(8,128)S(1)} %pad_maximum_fusion), channel_id=1, source_target_pairs={{0,1},{1,0},{2,3},{3,2},{4,5},{5,4},{6,7},{7,6},{8,9},{9,8},{10,11... | collective-permute-start | bytes 98312 | tf_op jit(solution)/shard_map/ppermute | solution.py:236
  7.5 7.8 %collective-permute-start.1 = (f32[256,128]{1,0:T(8,128)S(1)}, f32[256,128]{1,0:T(8,128)S(1)}, u32[]{:S(2)}, u32[]{:S(2)}) collective-permute-start(f32[256,128]{1,0:T(8,128)S(1)} %get-tuple-element.23.refs_1_), channel_id=1, source_target_pairs={{0,6},{1,7},{2,4},{3,5},{4,2},{5,3},{6,0},{7,1},{8,14},{9,15},{10,... | collective-permute-start | bytes 393224 | tf_op jit(solution)/shard_map/ppermute | solution.py:230
  12.2 6.0 %collective-permute-start.2 = (f32[256,128]{1,0:T(8,128)S(1)}, f32[256,128]{1,0:T(8,128)S(1)}, u32[]{:S(2)}, u32[]{:S(2)}) collective-permute-start(f32[256,128]{1,0:T(8,128)S(1)} %leaf_sums.5.refs_1_), channel_id=1, source_target_pairs={{0,2},{1,3},{2,0},{3,1},{4,6},{5,7},{6,4},{7,5},{8,10},{9,11},{10,... | collective-permute-start | bytes 393224 | tf_op jit(solution)/shard_map/ppermute | solution.py:230
  14.0 5.4 %collective-permute-start.3 = (f32[256,128]{1,0:T(8,128)S(1)}, f32[256,128]{1,0:T(8,128)S(1)}, u32[]{:S(2)}, u32[]{:S(2)}) collective-permute-start(f32[256,128]{1,0:T(8,128)S(1)} %leaf_sums.6.refs_1_), channel_id=1, source_target_pairs={{0,4},{1,5},{2,6},{3,7},{4,0},{5,1},{6,2},{7,3},{8,12},{9,13},{10,... | collective-permute-start | bytes 393224 | tf_op jit(solution)/shard_map/ppermute | solution.py:230
  19.4 5.2 %collective-permute-start.4 = (f32[256,128]{1,0:T(8,128)S(1)}, f32[256,128]{1,0:T(8,128)S(1)}, u32[]{:S(2)}, u32[]{:S(2)}) collective-permute-start(f32[256,128]{1,0:T(8,128)S(1)} %add.23), channel_id=1, source_target_pairs={{0,8},{1,17},{2,10},{3,19},{4,12},{5,21},{6,14},{7,23},{8,0},{9,25... | collective-permute-start | bytes 393224 | tf_op jit(solution)/shard_map/ppermute | solution.py:230
  24.6 5.9 %collective-permute-start.5 = (f32[256,128]{1,0:T(8,128)S(1)}, f32[256,128]{1,0:T(8,128)S(1)}, u32[]{:S(2)}, u32[]{:S(2)}) collective-permute-start(f32[256,128]{1,0:T(8,128)S(1)} %add.24), channel_id=1, source_target_pairs={{0,16},{1,9},{2,18},{3,11},{4,20},{5,13},{6,22},{7,15},{8,24},{9,1... | collective-permute-start | bytes 393224 | tf_op jit(solution)/shard_map/ppermute | solution.py:230
  30.5 5.2 %collective-permute-start.8 = (f32[128,128]{1,0:T(8,128)S(1)}, f32[128,128]{1,0:T(8,128)S(1)}, u32[]{:S(2)}, u32[]{:S(2)}) collective-permute-start(f32[128,128]{1,0:T(8,128)S(1)} %fusion.refs_0_), channel_id=1, source_target_pairs={{0,6},{1,7},{2,4},{3,5},{4,2},{5,3},{6,0},{7,1},{8,14},{9,15},{10,... | collective-permute-start | bytes 196616 | tf_op jit(solution)/shard_map/ppermute | solution.py:230
  32.2 5.2 %collective-permute-start.6 = (f32[128,128]{1,0:T(8,128)S(1)}, f32[128,128]{1,0:T(8,128)S(1)}, u32[]{:S(2)}, u32[]{:S(2)}) collective-permute-start(f32[128,128]{1,0:T(8,128)S(1)} %fusion.refs_0_), channel_id=1, source_target_pairs={{0,2},{1,3},{2,0},{3,1},{4,6},{5,7},{6,4},{7,5},{8,10},{9,11},{10,... | collective-permute-start | bytes 196616 | tf_op jit(solution)/shard_map/ppermute | solution.py:230
  32.6 4.9 %collective-permute-start.7 = (f32[128,128]{1,0:T(8,128)S(1)}, f32[128,128]{1,0:T(8,128)S(1)}, u32[]{:S(2)}, u32[]{:S(2)}) collective-permute-start(f32[128,128]{1,0:T(8,128)S(1)} %fusion.refs_0_), channel_id=1, source_target_pairs={{0,4},{1,5},{2,6},{3,7},{4,0},{5,1},{6,2},{7,3},{8,12},{9,13},{10,... | collective-permute-start | bytes 196616 | tf_op jit(solution)/shard_map/ppermute | solution.py:230

commit v6 on v5

--- a/solution.py
+++ b/solution.py
@@ -256,14 +256,15 @@
         for far in ((4, 8), (8, 4)):
             sums = sums + swap(sums, far)
         value = newton(sums)
-        values = [swap(value, far) for far in order[:3]] + [value]
+        gather = [(1, 1), (2, 2), (3, 3)]
+        values = [value] + [swap(value, far) for far in gather]
+        where = [(planes, far) for far in [(0, 0)] + gather]
     else:
         values = [newton(s) for s in lax.psum(parts, "rows")]
 
     if planes:
-        held = apply_blocks(where[3:], values[3:], x, hot_rows)
-        held = apply_blocks(where[:1], values[:1], x, hot_rows, held)
-        held = apply_blocks(where[1:3], values[1:3], x, hot_rows, held)
+        held = apply_blocks(where[:2], values[:2], x, hot_rows)
+        held = apply_blocks(where[2:], values[2:], x, hot_rows, held)
     else:
         held = apply_blocks(where, values, x, hot_rows)
     return held[0], held[1]

time: 40.3 us -> 40.4 us (level)
  waiting for transfers between devices: 10.6 us -> 11.5 us
  Pallas kernels: 15.7 us -> 14.9 us
    ppermute x8, waiting for transfers between devices: 10.6 us -> 11.5 us  [swap(): return lax.ppermute(value, ('rows', 'cls'), pairs)]
    pallas_call x3 -> x2, Pallas kernels: 5.9 us -> 5.11 us  [apply_blocks(): pl.pallas_call(functools.partial(apply_body, first, sizes, places), out_s...]
  transfers between devices with their start and end apart: 9 -> 9, of which waited for: 4 -> 6; matrix products, arithmetic and copies ran while one was open for 0% -> 0% of each run, Pallas kernels for 20% -> 18%
where the time goes in v6:
time: 40.4 us; the launch traced here: 40.1 us
  Pallas kernels  14.9 us (37%)
  starting transfers between devices  12.8 us (32%)
  waiting for transfers between devices  11.5 us (28%)
  between operations  0.77 us (2%)
    ppermute x8, starting transfers between devices, swap(): return lax.ppermute(value, ('rows', 'cls'), pairs)  12.3 us
    ppermute x8, waiting for transfers between devices, swap(): return lax.ppermute(value, ('rows', 'cls'), pairs)  11.5 us
    pallas_call x2, Pallas kernels, apply_blocks(): pl.pallas_call(functools.partial(apply_body, first, sizes, places), out_s...  5.11 us
    pallas_call x4, Pallas kernels, leaf_sums(): pl.pallas_call(functools.partial(sums_body, first, len(more) // 2, place)...  4.72 us
    pallas_call x1, Pallas kernels, local_stats(): pl.pallas_call(functools.partial(stats_body, chunks), out_shape=[full, fu...  3.88 us
    pallas_call x1, Pallas kernels, index_forms(): pl.pallas_call(functools.partial(index_body, width), out_shape=[pltpu.VME...  1.18 us
  transfers between devices with their start and end apart: 9, of which 6 were waited for; matrix products, arithmetic and copies ran while one was open for 0% of the time, Pallas kernels for 18%

profile of v6, /device:TPU:0, one launch (start us, length us, event | category | flops | bytes accessed | tf_op | source)
XLA Modules:
  0.0 40.1 jit_solution(15608298416043546129)
XLA Ops:
  0.6 0.0 copy-start.1
  0.6 0.0 copy-start
  0.6 3.9 %local_stats.1 = (f32[4096,512]{1,0:T(8,128)S(1)}, f32[4096,512]{1,0:T(8,128)S(1)}, f32[32,128]{1,0:T(8,128)S(1)}, f32[32,128]{1,0:T(8,128)S(1)}) custom-call(f32[4096,512]{1,0:T(8,128)} %x_hbm.1), custom_call_target="tpu_custom_call" | custom-call | flops 12582912 | bytes 8388608 | tf_op jit(solution)/shard_map/local_stats/pallas_call | solution.py:57
  4.5 0.5 %collective-permute-start = (f32[2,32,128]{2,1,0:T(8,128)S(1)}, f32[2,32,128]{2,1,0:T(8,128)S(1)}, u32[]{:S(2)}, u32[]{:S(2)}) collective-permute-start(f32[2,32,128]{2,1,0:T(8,128)S(1)} %pad_maximum_fusion), channel_id=1, source_target_pairs={{0,1},{1,0},{2,3},{3,2},{4,5},{5,4},{6,7},{7,6},{8,9},{9,8},{10,11... | collective-permute-start | bytes 98312 | tf_op jit(solution)/shard_map/ppermute | solution.py:236
  5.1 0.0 copy-done.1
  5.1 0.0 copy-done
  5.1 1.2 %index_forms.1 = (bf16[128,4096]{1,0:T(8,128)(2,1)S(1)}, bf16[4096,128]{1,0:T(8,128)(2,1)S(1)}, s32[4096,128]{1,0:T(8,128)S(1)}) custom-call(s32[32,128]{1,0:T(8,128)S(1)} %bitcast.10, s32[32,128]{1,0:T(8,128)S(1)} %bitcast.11), custom_call_target="tpu_custom_call" | custom-call | tf_op jit(solution)/shard_map/index_forms/pallas_call | solution.py:85
  6.3 0.0 collective-permute-done
  6.3 1.2 %leaf_sums.4 = (f32[256,128]{1,0:T(8,128)S(1)}, f32[4096,128]{1,0:T(8,128)S(1)}) custom-call(f32[4096,512]{1,0:T(8,128)S(1)} %get-tuple-element.15.e_ref, bf16[128,4096]{1,0:T(8,128)(2,1)S(1)} %get-tuple-element.16.hot_ref, s32[4096,128]{1,0:T(8,128)S(1)} %get-tuple-element.17.class_ref, f32[32,128]{1,0:T(8,128)S(1)} %get-tuple-element.18.refs_0_, ...), custom_call_target="tpu_custom_call" | custom-call | flops 1 | bytes 1 | tf_op jit(solution)/shard_map/leaf_sums/pallas_call | solution.py:148
  7.5 3.5 %collective-permute-start.1 = (f32[256,128]{1,0:T(8,128)S(1)}, f32[256,128]{1,0:T(8,128)S(1)}, u32[]{:S(2)}, u32[]{:S(2)}) collective-permute-start(f32[256,128]{1,0:T(8,128)S(1)} %get-tuple-element.21.refs_1_), channel_id=1, source_target_pairs={{0,6},{1,7},{2,4},{3,5},{4,2},{5,3},{6,0},{7,1},{8,14},{9,15},{10,... | collective-permute-start | bytes 393224 | tf_op jit(solution)/shard_map/ppermute | solution.py:230
  11.0 1.1 %leaf_sums.5.refs_1_ = f32[256,128]{1,0:T(8,128)S(1)} custom-call(f32[4096,512]{1,0:T(8,128)S(1)} %get-tuple-element.15.e_ref, bf16[128,4096]{1,0:T(8,128)(2,1)S(1)} %get-tuple-element.16.hot_ref, s32[4096,128]{1,0:T(8,128)S(1)} %get-tuple-element.17.class_ref, f32[4096,128]{1,0:T(8,128)S(1)} %get-tuple-element.20.refs_0_, ...), custom_call_target="tpu_custom_call" | custom-call | flops 1 | bytes 1 | tf_op jit(solution)/shard_map/leaf_sums/pallas_call | solution.py:148
  12.2 0.6 %collective-permute-start.2 = (f32[256,128]{1,0:T(8,128)S(1)}, f32[256,128]{1,0:T(8,128)S(1)}, u32[]{:S(2)}, u32[]{:S(2)}) collective-permute-start(f32[256,128]{1,0:T(8,128)S(1)} %leaf_sums.5.refs_1_), channel_id=1, source_target_pairs={{0,2},{1,3},{2,0},{3,1},{4,6},{5,7},{6,4},{7,5},{8,10},{9,11},{10,... | collective-permute-start | bytes 393224 | tf_op jit(solution)/shard_map/ppermute | solution.py:230
  12.7 1.2 %leaf_sums.6.refs_1_ = f32[256,128]{1,0:T(8,128)S(1)} custom-call(f32[4096,512]{1,0:T(8,128)S(1)} %get-tuple-element.15.e_ref, bf16[128,4096]{1,0:T(8,128)(2,1)S(1)} %get-tuple-element.16.hot_ref, s32[4096,128]{1,0:T(8,128)S(1)} %get-tuple-element.17.class_ref, f32[4096,128]{1,0:T(8,128)S(1)} %get-tuple-element.20.refs_0_, f32[256,128]{1,0:T(8,128)S(1)} %leaf_sums.5.refs_1_), custom_call_target="tpu_custom_call" | custom-call | flops 1 | bytes 1 | tf_op jit(solution)/shard_map/leaf_sums/pallas_call | solution.py:148
  14.0 0.1 collective-permute-start.3
  14.1 1.1 %leaf_sums.7 = f32[256,128]{1,0:T(8,128)S(1)} custom-call(f32[4096,512]{1,0:T(8,128)S(1)} %get-tuple-element.15.e_ref, bf16[128,4096]{1,0:T(8,128)(2,1)S(1)} %get-tuple-element.16.hot_ref, s32[4096,128]{1,0:T(8,128)S(1)} %get-tuple-element.17.class_ref, f32[4096,128]{1,0:T(8,128)S(1)} %get-tuple-element.20.refs_0_, f32[256,128]{1,0:T(8,128)S(1)} %leaf_sums.6.refs_1_), custom_call_target="tpu_custom_call" | custom-call | flops 1 | bytes 1 | tf_op jit(solution)/shard_map/leaf_sums/pallas_call | solution.py:148
  15.3 0.0 collective-permute-done.1
  15.3 2.9 %collective-permute-done.2 = f32[256,128]{1,0:T(8,128)S(1)} collective-permute-done((f32[256,128]{1,0:T(8,128)S(1)}, f32[256,128]{1,0:T(8,128)S(1)}, u32[]{:S(2)}, u32[]{:S(2)}) %collective-permute-start.2) | collective-permute-done | bytes 131104 | tf_op jit(solution)/shard_map/ppermute | solution.py:230
  18.2 1.2 %collective-permute-done.3 = f32[256,128]{1,0:T(8,128)S(1)} collective-permute-done((f32[256,128]{1,0:T(8,128)S(1)}, f32[256,128]{1,0:T(8,128)S(1)}, u32[]{:S(2)}, u32[]{:S(2)}) %collective-permute-start.3) | collective-permute-done | bytes 131104 | tf_op jit(solution)/shard_map/ppermute | solution.py:230
  19.4 1.6 %collective-permute-start.4 = (f32[256,128]{1,0:T(8,128)S(1)}, f32[256,128]{1,0:T(8,128)S(1)}, u32[]{:S(2)}, u32[]{:S(2)}) collective-permute-start(f32[256,128]{1,0:T(8,128)S(1)} %add.23), channel_id=1, source_target_pairs={{0,8},{1,17},{2,10},{3,19},{4,12},{5,21},{6,14},{7,23},{8,0},{9,25... | collective-permute-start | bytes 393224 | tf_op jit(solution)/shard_map/ppermute | solution.py:230
  21.0 3.5 %collective-permute-done.4 = f32[256,128]{1,0:T(8,128)S(1)} collective-permute-done((f32[256,128]{1,0:T(8,128)S(1)}, f32[256,128]{1,0:T(8,128)S(1)}, u32[]{:S(2)}, u32[]{:S(2)}) %collective-permute-start.4) | collective-permute-done | bytes 131104 | tf_op jit(solution)/shard_map/ppermute | solution.py:230
  24.6 2.9 %collective-permute-start.5 = (f32[256,128]{1,0:T(8,128)S(1)}, f32[256,128]{1,0:T(8,128)S(1)}, u32[]{:S(2)}, u32[]{:S(2)}) collective-permute-start(f32[256,128]{1,0:T(8,128)S(1)} %add.24), channel_id=1, source_target_pairs={{0,16},{1,9},{2,18},{3,11},{4,20},{5,13},{6,22},{7,15},{8,24},{9,1... | collective-permute-start | bytes 393224 | tf_op jit(solution)/shard_map/ppermute | solution.py:230
  27.5 3.0 %collective-permute-done.5 = f32[256,128]{1,0:T(8,128)S(1)} collective-permute-done((f32[256,128]{1,0:T(8,128)S(1)}, f32[256,128]{1,0:T(8,128)S(1)}, u32[]{:S(2)}, u32[]{:S(2)}) %collective-permute-start.5) | collective-permute-done | bytes 131104 | tf_op jit(solution)/shard_map/ppermute | solution.py:230
  30.5 1.5 %collective-permute-start.8 = (f32[128,128]{1,0:T(8,128)S(1)}, f32[128,128]{1,0:T(8,128)S(1)}, u32[]{:S(2)}, u32[]{:S(2)}) collective-permute-start(f32[128,128]{1,0:T(8,128)S(1)} %fusion.refs_0_), channel_id=1, source_target_pairs={{0,2},{1,3},{2,0},{3,1},{4,6},{5,7},{6,4},{7,5},{8,10},{9,11},{10,... | collective-permute-start | bytes 196616 | tf_op jit(solution)/shard_map/ppermute | solution.py:230
  32.1 0.5 %collective-permute-start.7 = (f32[128,128]{1,0:T(8,128)S(1)}, f32[128,128]{1,0:T(8,128)S(1)}, u32[]{:S(2)}, u32[]{:S(2)}) collective-permute-start(f32[128,128]{1,0:T(8,128)S(1)} %fusion.refs_0_), channel_id=1, source_target_pairs={{0,6},{1,7},{2,4},{3,5},{4,2},{5,3},{6,0},{7,1},{8,14},{9,15},{10,... | collective-permute-start | bytes 196616 | tf_op jit(solution)/shard_map/ppermute | solution.py:230
  32.6 1.5 %collective-permute-start.6 = (f32[128,128]{1,0:T(8,128)S(1)}, f32[128,128]{1,0:T(8,128)S(1)}, u32[]{:S(2)}, u32[]{:S(2)}) collective-permute-start(f32[128,128]{1,0:T(8,128)S(1)} %fusion.refs_0_), channel_id=1, source_target_pairs={{0,4},{1,5},{2,6},{3,7},{4,0},{5,1},{6,2},{7,3},{8,12},{9,13},{10,... | collective-permute-start | bytes 196616 | tf_op jit(solution)/shard_map/ppermute | solution.py:230
  34.1 0.8 %collective-permute-done.8.refs_1_ = f32[128,128]{1,0:T(8,128)S(1)} collective-permute-done((f32[128,128]{1,0:T(8,128)S(1)}, f32[128,128]{1,0:T(8,128)S(1)}, u32[]{:S(2)}, u32[]{:S(2)}) %collective-permute-start.8) | collective-permute-done | bytes 65568 | tf_op jit(solution)/shard_map/ppermute | solution.py:230
  34.9 2.6 %apply_blocks.2 = (f32[128,512]{1,0:T(8,128)}, f32[4096,512]{1,0:T(8,128)}) custom-call(f32[4096,512]{1,0:T(8,128)S(1)} %get-tuple-element.13.x_ref, bf16[4096,128]{1,0:T(8,128)(2,1)S(1)} %get-tuple-element.14.hot_ref, f32[128,128]{1,0:T(8,128)S(1)} %fusion.refs_0_, f32[128,128]{1,0:T(8,128)S(1)} %collective-permute-done.8.refs_1_), custom_call_target="tpu_custom_call" | custom-call | flops 536870912 | bytes 4194304 | tf_op jit(solution)/shard_map/apply_blocks/pallas_call | solution.py:201
  37.4 0.0 collective-permute-done.7.refs_1_
  37.4 0.1 collective-permute-done.6.refs_0_
  37.6 2.5 %apply_blocks.3 = (f32[128,512]{1,0:T(8,128)}, f32[4096,512]{1,0:T(8,128)}) custom-call(f32[4096,512]{1,0:T(8,128)S(1)} %get-tuple-element.13.x_ref, bf16[4096,128]{1,0:T(8,128)(2,1)S(1)} %get-tuple-element.14.hot_ref, f32[128,128]{1,0:T(8,128)S(1)} %collective-permute-done.6.refs_0_, ...), custom_call_target="tpu_custom_call", output_to_operand_aliasing={{0}: (4, {}), {1}: (5, {})} | custom-call | flops 536870912 | bytes 4194304 | tf_op jit(solution)/shard_map/apply_blocks/pallas_call | solution.py:201
  (8 shorter events, 0.1 us)
Async XLA Ops:
  0.6 4.4 %copy-start.1 = (s32[4096]{0:T(1024)S(1)}, s32[4096]{0:T(1024)}, u32[]{:S(2)}) copy-start(s32[4096]{0:T(1024)} %param.5) | copy-start | bytes 49156
  0.6 4.4 %copy-start = (s32[4096]{0:T(1024)S(1)}, s32[4096]{0:T(1024)}, u32[]{:S(2)}) copy-start(s32[4096]{0:T(1024)} %param.4) | copy-start | bytes 49156
  4.5 1.7 %collective-permute-start = (f32[2,32,128]{2,1,0:T(8,128)S(1)}, f32[2,32,128]{2,1,0:T(8,128)S(1)}, u32[]{:S(2)}, u32[]{:S(2)}) collective-permute-start(f32[2,32,128]{2,1,0:T(8,128)S(1)} %pad_maximum_fusion), channel_id=1, source_target_pairs={{0,1},{1,0},{2,3},{3,2},{4,5},{5,4},{6,7},{7,6},{8,9},{9,8},{10,11... | collective-permute-start | bytes 98312 | tf_op jit(solution)/shard_map/ppermute | solution.py:236
  7.5 7.8 %collective-permute-start.1 = (f32[256,128]{1,0:T(8,128)S(1)}, f32[256,128]{1,0:T(8,128)S(1)}, u32[]{:S(2)}, u32[]{:S(2)}) collective-permute-start(f32[256,128]{1,0:T(8,128)S(1)} %get-tuple-element.21.refs_1_), channel_id=1, source_target_pairs={{0,6},{1,7},{2,4},{3,5},{4,2},{5,3},{6,0},{7,1},{8,14},{9,15},{10,... | collective-permute-start | bytes 393224 | tf_op jit(solution)/shard_map/ppermute | solution.py:230
  12.2 6.0 %collective-permute-start.2 = (f32[256,128]{1,0:T(8,128)S(1)}, f32[256,128]{1,0:T(8,128)S(1)}, u32[]{:S(2)}, u32[]{:S(2)}) collective-permute-start(f32[256,128]{1,0:T(8,128)S(1)} %leaf_sums.5.refs_1_), channel_id=1, source_target_pairs={{0,2},{1,3},{2,0},{3,1},{4,6},{5,7},{6,4},{7,5},{8,10},{9,11},{10,... | collective-permute-start | bytes 393224 | tf_op jit(solution)/shard_map/ppermute | solution.py:230
  14.0 5.4 %collective-permute-start.3 = (f32[256,128]{1,0:T(8,128)S(1)}, f32[256,128]{1,0:T(8,128)S(1)}, u32[]{:S(2)}, u32[]{:S(2)}) collective-permute-start(f32[256,128]{1,0:T(8,128)S(1)} %leaf_sums.6.refs_1_), channel_id=1, source_target_pairs={{0,4},{1,5},{2,6},{3,7},{4,0},{5,1},{6,2},{7,3},{8,12},{9,13},{10,... | collective-permute-start | bytes 393224 | tf_op jit(solution)/shard_map/ppermute | solution.py:230
  19.4 5.2 %collective-permute-start.4 = (f32[256,128]{1,0:T(8,128)S(1)}, f32[256,128]{1,0:T(8,128)S(1)}, u32[]{:S(2)}, u32[]{:S(2)}) collective-permute-start(f32[256,128]{1,0:T(8,128)S(1)} %add.23), channel_id=1, source_target_pairs={{0,8},{1,17},{2,10},{3,19},{4,12},{5,21},{6,14},{7,23},{8,0},{9,25... | collective-permute-start | bytes 393224 | tf_op jit(solution)/shard_map/ppermute | solution.py:230
  24.6 5.9 %collective-permute-start.5 = (f32[256,128]{1,0:T(8,128)S(1)}, f32[256,128]{1,0:T(8,128)S(1)}, u32[]{:S(2)}, u32[]{:S(2)}) collective-permute-start(f32[256,128]{1,0:T(8,128)S(1)} %add.24), channel_id=1, source_target_pairs={{0,16},{1,9},{2,18},{3,11},{4,20},{5,13},{6,22},{7,15},{8,24},{9,1... | collective-permute-start | bytes 393224 | tf_op jit(solution)/shard_map/ppermute | solution.py:230
  30.5 4.3 %collective-permute-start.8 = (f32[128,128]{1,0:T(8,128)S(1)}, f32[128,128]{1,0:T(8,128)S(1)}, u32[]{:S(2)}, u32[]{:S(2)}) collective-permute-start(f32[128,128]{1,0:T(8,128)S(1)} %fusion.refs_0_), channel_id=1, source_target_pairs={{0,2},{1,3},{2,0},{3,1},{4,6},{5,7},{6,4},{7,5},{8,10},{9,11},{10,... | collective-permute-start | bytes 196616 | tf_op jit(solution)/shard_map/ppermute | solution.py:230
  32.1 5.4 %collective-permute-start.7 = (f32[128,128]{1,0:T(8,128)S(1)}, f32[128,128]{1,0:T(8,128)S(1)}, u32[]{:S(2)}, u32[]{:S(2)}) collective-permute-start(f32[128,128]{1,0:T(8,128)S(1)} %fusion.refs_0_), channel_id=1, source_target_pairs={{0,6},{1,7},{2,4},{3,5},{4,2},{5,3},{6,0},{7,1},{8,14},{9,15},{10,... | collective-permute-start | bytes 196616 | tf_op jit(solution)/shard_map/ppermute | solution.py:230
  32.6 5.0 %collective-permute-start.6 = (f32[128,128]{1,0:T(8,128)S(1)}, f32[128,128]{1,0:T(8,128)S(1)}, u32[]{:S(2)}, u32[]{:S(2)}) collective-permute-start(f32[128,128]{1,0:T(8,128)S(1)} %fusion.refs_0_), channel_id=1, source_target_pairs={{0,4},{1,5},{2,6},{3,7},{4,0},{5,1},{6,2},{7,3},{8,12},{9,13},{10,... | collective-permute-start | bytes 196616 | tf_op jit(solution)/shard_map/ppermute | solution.py:230
